TPU v7x, 256 devices: a whole 4x4x8 slice. The times are simulated.
256 devices in a mesh: tm: 8 (over x, z_lo), lat: 32 (over y, z_hi, core).
Axes of the slice: x: 4, y: 4, z: 8 (z_hi: 4, z_lo: 2; z = z_hi * 2 + z_lo), core: 2. Of those that a mesh axis runs over, the one named last changes fastest.
Arguments:
- starts: float32 [8, 3, 8, 512, 512], P('tm', None, None, 'lat'), may hold values from -1.2 to 1.2
- coarse_old: float32 [8, 3, 8, 256, 256], P('tm', None, None, 'lat'), may hold values from -1.2 to 1.2
- mean_depth: float32 [8], replicated, may hold values from 0.5 to 2
- coupling: float32 [8, 8], replicated, may hold values from 0 to 1, as said below
- wet_cells: int32 [512, 512], P('lat'), may hold values 0 or 1
Outputs:
- new_ends: float32 [8, 3, 8, 512, 512], P('tm', None, None, 'lat')
- coarse_new: float32 [8, 3, 8, 256, 256], P('tm', None, None, 'lat')
Inputs may be any that keep to these rules, and one draw needn't show every extreme that they name: `coupling`: symmetric; each diagonal entry is at least 0.6 and exceeds the sum of magnitudes of the other entries of its row.
All inputs are finite; a program needn't handle non-finite values. No bound on the sum of `wet_cells` on one device may be relied on, other than what follows from the above.
Results may differ from a plain program's by a relative error of at most 0.00012.
Values sent between devices are 32-bit elements; how exact they have to be, the bound alone decides.
A program may use at most 128 MiB of HBM per device.

v0:
```python
import functools

import jax
import jax.numpy as jnp
from jax import lax
from jax.experimental import pallas as pl
from jax.experimental.pallas import tpu as pltpu
from jax.sharding import PartitionSpec as P

MESH = pl.DeviceIdType.MESH
F32 = jnp.float32

STEPS = 4
time_step = 0.15
viscosity = 0.02
rotation = 0.3

HALO = 3


def iota(shape, dim):
    return lax.broadcasted_iota(jnp.int32, shape, dim)


def dot(a, b):
    return jnp.dot(a, b, precision=lax.Precision.HIGHEST, preferred_element_type=F32)


def rolled(x, shift):
    return pltpu.roll(x, shift % x.shape[-1], axis=x.ndim - 1)


def updated(src, r, p, depth, wet, f, spacing, old, weights, step, inside):
    k = viscosity / (spacing * spacing)
    half = 0.5 / spacing
    e, u, v = src[r, 0], src[r, 1], src[r, 2]
    un, us = src[r + 1, 1], src[r - 1, 1]
    vn, vs = src[r + 1, 2], src[r - 1, 2]
    hvn = (depth + src[r + 1, 0]) * vn
    hvs = (depth + src[r - 1, 0]) * vs
    hu = (depth + e) * u
    pc = p[r]
    ue, uw = rolled(u, -1), rolled(u, 1)
    ve, vw = rolled(v, -1), rolled(v, 1)
    u2, v2 = u * half, v * half
    east, west, north, south = k - u2, k + u2, k - v2, k + v2
    zu = (ue * east + uw * west) + (un * north + us * south)
    zv = (ve * east + vw * west) + (vn * north + vs * south)
    zu = zu + (f * v - (4.0 * k) * u) - (rolled(pc, -1) - rolled(pc, 1))
    zv = zv - (f * u + (4.0 * k) * v) - (p[r + 1] - p[r - 1])
    ze = (rolled(hu, -1) - rolled(hu, 1)) + (hvn - hvs)
    w = wet * step
    ce = jnp.where(inside, -step * half, 0.0).astype(F32)
    out = [ce * ze, w * zu, w * zv]
    first, second = weights
    now = [e, u, v]
    for i in range(3):
        out[i] = out[i] + (now[i] if second == 1.0 else second * now[i])
        if first != 0.0:
            out[i] = out[i] + first * old[r, i]
    return out


def kernel(NT, NL, starts, coarse_old, mean_depth, coupling, wet_cells, ends, coarse_new,
           YA, Y1, Y2, PB, WET, WX, HB, KF, KC, WW, W2, WR, WP, DL, TX, RX, TC, RC, CT, PC, WC, RES,
           CO, BW, CN, C0, P0, W0,
           hs_send, hs_recv, wx_send, wx_recv, tx_send, rx_recv, tc_send, rc_recv):
    R, W = wet_cells.shape
    L = 8
    RC_ROWS, WCO = R // 2, W // 2
    SLAB = WCO // NT
    n, q = lax.axis_index("tm"), lax.axis_index("lat")
    up, down = q > 0, q < NL - 1
    inside_side = {-1: up, 1: down}

    barrier = pltpu.get_barrier_semaphore()

    def greet(m, row):
        pl.semaphore_signal(barrier, inc=1, device_id=(m, row), device_id_type=MESH)

    for j in range(1, NT):
        greet(lax.rem(n + j, NT), q)
    for d in (-1, 1):
        @pl.when(inside_side[d])
        def _(d=d):
            for j in range(NT):
                greet(lax.rem(n + j, NT), q + d)

    for f in range(3):
        for b in range(R // 8):
            YA[pl.ds(HALO + 8 * b, 8), f] = jnp.swapaxes(starts[f, :, pl.ds(8 * b, 8), :], 0, 1)

    pl.semaphore_wait(barrier, (NT - 1) + NT * up.astype(jnp.int32) + NT * down.astype(jnp.int32))

    def halo_copy(k, side):
        first = HALO if side == -1 else R
        slot = 1 if side == -1 else 0
        return pltpu.make_async_remote_copy(
            src_ref=YA.at[pl.ds(first, HALO)], dst_ref=HB.at[k, slot],
            send_sem=hs_send.at[k, slot], recv_sem=hs_recv.at[k, slot],
            device_id=(n, q + side), device_id_type=MESH)

    def halo_arrival(k, slot, side):
        return pltpu.make_async_remote_copy(
            src_ref=YA.at[pl.ds(0, HALO)], dst_ref=HB.at[k, slot],
            send_sem=hs_send.at[k, slot], recv_sem=hs_recv.at[k, slot],
            device_id=(n, q + side), device_id_type=MESH)

    def wet_copy(side):
        slot = 1 if side == -1 else 0
        return pltpu.make_async_remote_copy(
            src_ref=wet_cells, dst_ref=WX.at[slot], send_sem=wx_send.at[slot], recv_sem=wx_recv.at[slot],
            device_id=(n, q + side), device_id_type=MESH)

    def send_halos(k):
        for side in (-1, 1):
            @pl.when(inside_side[side])
            def _(side=side):
                halo_copy(k, side).start()

    send_halos(0)
    for side in (-1, 1):
        @pl.when(inside_side[side])
        def _(side=side):
            wet_copy(side).start()

        @pl.when(jnp.logical_not(inside_side[side]))
        def _(side=side):
            slot = 0 if side == -1 else 1
            WX[slot] = jnp.zeros((R, W), jnp.int32)
            YA[pl.ds(0 if side == -1 else HALO + R, HALO)] = jnp.zeros((HALO, 3, L, W), F32)
            RX[:, pl.ds(0 if side == -1 else RC_ROWS, RC_ROWS // 2)] = jnp.zeros(
                (NT - 1, RC_ROWS // 2, 3, L, 128), F32)

    KN = KF.shape[0]
    spread = (iota((KN, L), 0) % L == iota((KN, L), 1)).astype(F32)
    spread_t = (iota((L, KN), 1) % L == iota((L, KN), 0)).astype(F32)
    blocks = dot(dot(spread, coupling[...]), spread_t)
    blocks = jnp.where(iota((KN, KN), 0) // L == iota((KN, KN), 1) // L, blocks, 0.0)
    KF[...] = 0.5 * blocks
    KC[...] = 0.25 * blocks

    def depth_of(width):
        rows = iota((L, width), 0)
        value = jnp.zeros((L, width), F32)
        for l in range(L):
            value = jnp.where(rows == l, mean_depth[l], value)
        return value

    wet_own = wet_cells[...].astype(F32)
    for r in range(R):
        WET[HALO + r] = jnp.broadcast_to(wet_own[r:r + 1, :], (L, W))

    target = (iota((W, W), 1) // 64 * SLAB - 16 + iota((W, W), 1) % 64 + WCO) % WCO
    WW[...] = (iota((W, W), 0) // 2 == target).astype(F32)
    W2[...] = (iota((WCO, W), 0) == target[:WCO]).astype(F32)
    WR[...] = (iota((W, WCO), 0) // 2 == iota((W, WCO), 1)).astype(F32)
    WP[...] = (iota((WCO, W), 1) // 2 == iota((WCO, W), 0)).astype(F32)

    @pl.when(n == 0)
    def _():
        sums = jnp.stack([YA[HALO + 2 * i] + YA[HALO + 1 + 2 * i] for i in range(RC_ROWS)])
        C0[pl.ds(1, RC_ROWS)] = (0.25 * dot(sums.reshape(-1, W), WR[...])).reshape(RC_ROWS, 3, L, WCO)

    for f in range(3):
        CO[:, f] = jnp.swapaxes(coarse_old[f], 0, 1)

    def fine_f(r):
        row = q * R + (r - HALO)
        return rotation * (2.0 * (row.astype(F32) + 0.5) / (R * NL) - 1.0), (row >= 0) & (row < R * NL)

    stages = (
        (YA, Y1, (0.0, 1.0), 1.0),
        (Y1, Y2, (0.75, 0.25), 0.25),
        (Y2, YA, (1.0 / 3.0, 2.0 / 3.0), 2.0 / 3.0),
    )

    def pressure(stage, pieces):
        src = stages[stage][0]
        count = sum(c for _, c in pieces)
        rows = [src[pl.ds(a, c), 0] for a, c in pieces]
        rows = rows[0] if len(rows) == 1 else jnp.concatenate(rows, axis=0)
        size = count * L
        result = dot(KF[pl.ds(0, size), pl.ds(0, size)], rows.reshape(size, W)).reshape(count, L, W)
        at = 0
        for a, c in pieces:
            PB[stage, pl.ds(a, c)] = result[at:at + c]
            at += c

    def fine_row(stage, r):
        src, dst, weights, g = stages[stage]
        f, inside = fine_f(r)
        new = updated(src, r, PB.at[stage], depth_of(W), WET[r], f, 1.0, YA, weights, g * time_step, inside)
        for i in range(3):
            dst[r, i] = new[i]

    def coarse_first():
        sums = jnp.stack([YA[1] + YA[2], YA[HALO + R] + YA[HALO + R + 1]])
        outer = (0.25 * dot(sums.reshape(-1, W), WR[...])).reshape(2, 3, L, WCO)
        C0[0] = outer[0]
        C0[RC_ROWS + 1] = outer[1]
        size = (RC_ROWS + 2) * L
        P0[...] = dot(KC[pl.ds(0, size), pl.ds(0, size)], C0[:, 0].reshape(size, WCO)).reshape(RC_ROWS + 2, L, WCO)
        pairs = (iota((RC_ROWS, R), 1) // 2 == iota((RC_ROWS, R), 0)).astype(F32)
        wet_full = (dot(dot(pairs, wet_cells[...].astype(F32)), WR[...]) > 3.5).astype(F32)
        for i in range(RC_ROWS):
            W0[i] = jnp.broadcast_to(wet_full[i:i + 1, :], (L, WCO))

        @pl.loop(1, RC_ROWS + 1)
        def _(r):
            row = q * RC_ROWS + r - 1
            f = rotation * (2.0 * (row.astype(F32) + 0.5) / (RC_ROWS * NL) - 1.0)
            new = updated(C0, r, P0, depth_of(WCO), W0[r - 1], f, 2.0, None, (0.0, 1.0), STEPS * time_step, True)
            for i in range(3):
                CN[r - 1, i] = new[i]

    @pl.loop(0, STEPS)
    def _(k):
        for stage in range(3):
            pressure(stage, [(HALO + stage, R - 2 * stage)])

            @pl.loop(0, (R - 2 * (stage + 1)) // 2)
            def _(j, stage=stage):
                for more in range(2):
                    fine_row(stage, HALO + stage + 1 + 2 * j + more)

        for side in (-1, 1):
            slot = 0 if side == -1 else 1

            @pl.when(inside_side[side])
            def _(side=side, slot=slot):
                halo_arrival(k, slot, side).wait_recv()
                YA[pl.ds(0 if side == -1 else HALO + R, HALO)] = HB[k, slot]
                halo_copy(k, side).wait_send()

        @pl.when(k == 0)
        def _():
            for side in (-1, 1):
                @pl.when(inside_side[side])
                def _(side=side):
                    wet_copy(side).wait_send()
                    wet_copy(-side).wait_recv()
            for r in range(HALO):
                WET[r] = jnp.broadcast_to(WX[0, R - HALO + r:R - HALO + r + 1, :].astype(F32), (L, W))
                WET[HALO + R + r] = jnp.broadcast_to(WX[1, r:r + 1, :].astype(F32), (L, W))

            @pl.when(n == 0)
            def _():
                coarse_first()
                BW[...] = dot((CN[...] - CO[...]).reshape(-1, WCO), W2[...])

            @pl.when(n > 0)
            def _():
                BW[...] = dot((-CO[...]).reshape(-1, WCO), W2[...])

        for stage in range(3):
            pressure(stage, [(stage, HALO), (HALO + R - stage, HALO)])

            @pl.loop(0, HALO)
            def _(j, stage=stage):
                fine_row(stage, stage + 1 + j)
                fine_row(stage, R - stage + 2 + j)

        @pl.when(k < STEPS - 1)
        def _():
            send_halos(k + 1)

    sums = jnp.stack([YA[HALO + 2 * i] + YA[HALO + 1 + 2 * i] for i in range(RC_ROWS)])
    DL[...] = (0.25 * dot(sums.reshape(-1, W), WW[...]) + BW[...]).reshape(RC_ROWS, 3, L, W)
    lanes = iota((L, 128), 1)
    for i in range(RC_ROWS // 2):
        for f in range(3):
            for j in range(NT // 2):
                a = DL[2 * i, f, :, pl.ds(128 * j, 128)]
                b = DL[2 * i + 1, f, :, pl.ds(128 * j, 128)]
                TX[2 * j, i, f] = jnp.where(lanes < 64, a, rolled(b, 64))
                TX[2 * j + 1, i, f] = jnp.where(lanes < 64, rolled(a, 64), b)

    HU = RC_ROWS // 2

    def delta_copy(m, d, units):
        first, to = {0: (0, HU), 1: (HU - units, HU - units), -1: (0, 2 * HU)}[d]
        return pltpu.make_async_remote_copy(
            src_ref=TX.at[m, pl.ds(first, units)], dst_ref=RX.at[n, pl.ds(to, units)],
            send_sem=tx_send.at[m, d + 1], recv_sem=rx_recv.at[n, d + 1],
            device_id=(m, q + d), device_id_type=MESH)

    def delta_arrival(s, d, units):
        to = {0: HU, 1: HU - units, -1: 2 * HU}[d]
        return pltpu.make_async_remote_copy(
            src_ref=TX.at[0, pl.ds(0, units)], dst_ref=RX.at[s, pl.ds(to, units)],
            send_sem=tx_send.at[0, d + 1], recv_sem=rx_recv.at[s, d + 1],
            device_id=(s, q - d), device_id_type=MESH)

    def for_deltas(act):
        for units in sorted({(NT - s) // 2 for s in range(NT - 1)}):
            @pl.when((n < NT - 1) & ((NT - n) // 2 == units))
            def _(units=units):
                @pl.loop(0, NT)
                def _(j):
                    m = lax.rem(n + j, NT)

                    @pl.when(down)
                    def _():
                        act(delta_copy(m, 1, units))

                    @pl.when(up)
                    def _():
                        act(delta_copy(m, -1, units))

                    @pl.when(j > 0)
                    def _():
                        act(delta_copy(m, 0, HU))

    for_deltas(lambda copy: copy.start())

    @pl.when(n < NT - 1)
    def _():
        RX[n, pl.ds(HU, HU)] = TX[n]

    E = 3 * RC_ROWS
    col = iota((W, 128), 1)
    own = (n * SLAB - 16 + col + WCO) % WCO
    picks = jnp.where((iota((W, 128), 0) // 2 == own) & (col < 64), 1.0, 0.0).astype(F32)
    pairs = (iota((RC_ROWS, R), 1) // 2 == iota((RC_ROWS, R), 0)).astype(F32)
    for part, cells in enumerate((WX[0], wet_cells[...], WX[1])):
        window = (dot(dot(pairs, cells.astype(F32)), picks) > 3.5).astype(F32)
        for i in range(RC_ROWS):
            WC[part * RC_ROWS + i] = jnp.broadcast_to(window[i:i + 1, :], (L, 128))

    def arrived(s):
        h = (NT - s) // 2

        @pl.when(up)
        def _():
            delta_arrival(s, 1, h).wait_recv()

        @pl.when(down)
        def _():
            delta_arrival(s, -1, h).wait_recv()

        @pl.when(n != s)
        def _():
            delta_arrival(s, 0, HU).wait_recv()

    def row_of(s, r, f):
        x = RX[s, r // 2, f]
        return x if r % 2 == 0 else rolled(x, 64)

    arrived(0)
    for r in range(E):
        for f in range(3):
            CT[0, r, f] = row_of(0, r, f)

    def result_copy(s):
        return pltpu.make_async_remote_copy(
            src_ref=TC.at[s], dst_ref=RC.at[n], send_sem=tc_send.at[s], recv_sem=rc_recv.at[n],
            device_id=(s, q), device_id_type=MESH)

    def result_arrival(m):
        return pltpu.make_async_remote_copy(
            src_ref=TC.at[0], dst_ref=RC.at[m], send_sem=tc_send.at[0], recv_sem=rc_recv.at[m],
            device_id=(m, q), device_id_type=MESH)

    depth = depth_of(128)
    group = lanes // SLAB
    for s in range(1, NT):
        now, later = CT.at[(s - 1) % 2], CT.at[s % 2]
        h = NT - 1 - s
        lo, hi = RC_ROWS - h, 2 * RC_ROWS + h
        size = (hi - lo + 2) * L
        PC[pl.ds(lo - 1, hi - lo + 2)] = dot(
            KC[pl.ds(0, size), pl.ds(0, size)], now[pl.ds(lo - 1, hi - lo + 2), 0].reshape(size, 128)
        ).reshape(hi - lo + 2, L, 128)
        if s < NT - 1:
            arrived(s)
        for r in range(lo, hi):
            row = q * RC_ROWS + (r - RC_ROWS)
            f = rotation * (2.0 * (row.astype(F32) + 0.5) / (RC_ROWS * NL) - 1.0)
            inside = (row >= 0) & (row < RC_ROWS * NL)
            new = updated(now, r, PC, depth, WC[r], f, 2.0, None, (0.0, 1.0), STEPS * time_step, inside)
            for i in range(3):
                if RC_ROWS <= r < 2 * RC_ROWS:
                    RES[r - RC_ROWS, i] = new[i]
                if s < NT - 1:
                    later[r, i] = new[i] + row_of(s, r, i)
        for b in range(2):
            for i in range(3):
                packed = rolled(RES[4 * b, i], -16)
                for g in range(1, 4):
                    packed = jnp.where(group == g, rolled(RES[4 * b + g, i], SLAB * g - 16), packed)
                TC[s, b, i] = packed

        @pl.when(n != s)
        def _(s=s):
            result_copy(s).start()

        @pl.when(n == s)
        def _(s=s):
            RC[s] = TC[s]

    @pl.when(n > 0)
    def _():
        @pl.loop(1, NT)
        def _(j):
            result_arrival(lax.rem(n + j, NT)).wait_recv()

        for r in range(RC_ROWS):
            b, g = r // 4, r % 4
            for i in range(3):
                for j in range(WCO // 128):
                    value = rolled(RC[4 * j, b, i], -SLAB * g)
                    for m in range(1, 4):
                        value = jnp.where(group == m, rolled(RC[4 * j + m, b, i], SLAB * (m - g)), value)
                    CN[r, i, :, pl.ds(128 * j, 128)] = value

    change = dot((CN[...] - CO[...]).reshape(-1, WCO), WP[...]).reshape(RC_ROWS, 3, L, W)
    for i in range(3):
        coarse_new[i] = jnp.swapaxes(CN[:, i], 0, 1)
    for r in range(RC_ROWS):
        for i in range(3):
            for more in range(2):
                YA[HALO + 2 * r + more, i] = YA[HALO + 2 * r + more, i] + change[r, i]
    for i in range(3):
        for b in range(R // 8):
            ends[i, :, pl.ds(8 * b, 8), :] = jnp.swapaxes(YA[pl.ds(HALO + 8 * b, 8), i], 0, 1)

    for_deltas(lambda copy: copy.wait_send())
    for s in range(1, NT):
        @pl.when(n != s)
        def _(s=s):
            result_copy(s).wait_send()


def local(NT, NL, starts, coarse_old, mean_depth, coupling, wet_cells):
    R, W = wet_cells.shape
    L = 8
    C, WCO = R // 2, W // 2
    E = R + 2 * HALO
    vmem = lambda *shape: pltpu.VMEM(shape, F32)
    sems = lambda *shape: pltpu.SemaphoreType.DMA(shape)
    space = pl.BlockSpec(memory_space=pltpu.VMEM)
    ends, coarse_new = pl.pallas_call(
        functools.partial(kernel, NT, NL),
        out_shape=(jax.ShapeDtypeStruct((3, L, R, W), F32), jax.ShapeDtypeStruct((3, L, C, WCO), F32)),
        in_specs=[space, space, pl.BlockSpec(memory_space=pltpu.SMEM), space, space],
        out_specs=(space, space),
        scratch_shapes=[
            vmem(E, 3, L, W), vmem(E, 3, L, W), vmem(E, 3, L, W), vmem(3, E, L, W), vmem(E, L, W),
            pltpu.VMEM((2, R, W), jnp.int32), vmem(STEPS, 2, HALO, 3, L, W),
            vmem(3 * C * L, 3 * C * L), vmem(3 * C * L, 3 * C * L),
            vmem(W, W), vmem(WCO, W), vmem(W, WCO), vmem(WCO, W), vmem(C, 3, L, W),
            vmem(NT, C // 2, 3, L, 128), vmem(NT - 1, 3 * C // 2, 3, L, 128),
            vmem(NT, 2, 3, L, 128), vmem(NT, 2, 3, L, 128),
            vmem(2, 3 * C, 3, L, 128), vmem(3 * C, L, 128), vmem(3 * C, L, 128), vmem(C, 3, L, 128),
            vmem(C, 3, L, WCO), vmem(C * 3 * L, W), vmem(C, 3, L, WCO),
            vmem(C + 2, 3, L, WCO), vmem(C + 2, L, WCO), vmem(C, L, WCO),
            sems(STEPS, 2), sems(STEPS, 2), sems(2), sems(2), sems(NT, 3), sems(NT - 1, 3), sems(NT), sems(NT),
        ],
        compiler_params=pltpu.CompilerParams(
            collective_id=0, has_side_effects=True, vmem_limit_bytes=48 * 1024 * 1024),
    )(starts[0], coarse_old[0], mean_depth, coupling, wet_cells)
    return ends[None], coarse_new[None]


def solution(mesh):
    NT, NL = mesh.shape["tm"], mesh.shape["lat"]
    in_specs = (
        P("tm", None, None, "lat", None),
        P("tm", None, None, "lat", None),
        P(),
        P(),
        P("lat", None),
    )
    out_specs = (P("tm", None, None, "lat", None), P("tm", None, None, "lat", None))
    return jax.shard_map(functools.partial(local, NT, NL), mesh=mesh, in_specs=in_specs, out_specs=out_specs,
                         check_vma=False)
```

profile of v0, /device:TPU:30, one launch (start us, length us, event | category | flops | bytes accessed | tf_op | source)
XLA Modules:
  0.0 74.6 jit_solution(12360557385764642398)
XLA Ops:
  0.6 0.0 copy-start.4
  0.6 0.6 copy-done.4
  1.3 0.0 copy-start
  1.3 1.1 %copy-done = f32[1,3,8,16,512]{4,3,2,1,0:T(8,128)S(1)} copy-done((f32[1,3,8,16,512]{4,3,2,1,0:T(8,128)S(1)}, f32[1,3,8,16,512]{4,3,2,1,0:T(8,128)}, u32[]{:S(2)}) %copy-start) | copy-done | bytes 786456
  2.4 0.0 copy-start.1
  2.4 0.9 %copy-done.1 = f32[1,3,8,8,256]{4,3,2,1,0:T(8,128)S(1)} copy-done((f32[1,3,8,8,256]{4,3,2,1,0:T(8,128)S(1)}, f32[1,3,8,8,256]{4,3,2,1,0:T(8,128)}, u32[]{:S(2)}) %copy-start.1) | copy-done | bytes 196632
  3.3 0.0 copy-start.2
  3.4 0.8 %copy-done.2 = s32[16,512]{1,0:T(8,128)S(1)} copy-done((s32[16,512]{1,0:T(8,128)S(1)}, s32[16,512]{1,0:T(8,128)}, u32[]{:S(2)}) %copy-start.2) | copy-done | bytes 32792
  4.1 0.0 copy-start.3
  4.1 0.7 copy-done.3
  4.8 68.2 %shard_map.68 = (f32[3,8,16,512]{3,2,1,0:T(8,128)S(1)}, f32[3,8,8,256]{3,2,1,0:T(8,128)S(1)}) custom-call(f32[3,8,16,512]{3,2,1,0:T(8,128)S(1)} %bitcast.4, f32[3,8,8,256]{3,2,1,0:T(8,128)S(1)} %bitcast.6, f32[8]{0:T(128)S(1)} %copy-done.4, f32[8,8]{1,0:T(8,128)S(1)} %copy-done.3, s32[16,512]{1,0:T(8,128)S(1)} %copy-done.2), custom_call_target="tpu_custom_call" | custom-call | tf_op jit(solution)/shard_map/pallas_call | solution.py:443
  73.0 0.9 %copy.9 = f32[1,3,8,16,512]{4,3,2,1,0:T(8,128)} copy(f32[1,3,8,16,512]{4,3,2,1,0:T(8,128)S(1)} %bitcast.5) | data formatting | bytes 1572864
  73.9 0.7 copy.10
Async XLA Ops:
  0.6 0.7 copy-start.4
  1.3 1.1 %copy-start = (f32[1,3,8,16,512]{4,3,2,1,0:T(8,128)S(1)}, f32[1,3,8,16,512]{4,3,2,1,0:T(8,128)}, u32[]{:S(2)}) copy-start(f32[1,3,8,16,512]{4,3,2,1,0:T(8,128)} %param.5) | copy-start | bytes 2359300
  2.4 0.9 %copy-start.1 = (f32[1,3,8,8,256]{4,3,2,1,0:T(8,128)S(1)}, f32[1,3,8,8,256]{4,3,2,1,0:T(8,128)}, u32[]{:S(2)}) copy-start(f32[1,3,8,8,256]{4,3,2,1,0:T(8,128)} %param.6) | copy-start | bytes 589828
  3.3 0.8 %copy-start.2 = (s32[16,512]{1,0:T(8,128)S(1)}, s32[16,512]{1,0:T(8,128)}, u32[]{:S(2)}) copy-start(s32[16,512]{1,0:T(8,128)} %wet_cells.1) | copy-start | bytes 98308
  4.1 0.7 copy-start.3
where the time goes:
time: 74.8 us; the launch traced here: 74.6 us
  Pallas kernels  68.2 us (91%)
  local copies, waits for them, and re-layouts  5.71 us (8%)
    pallas_call x1, Pallas kernels, local(): pl.pallas_call(functools.partial(kernel, NT, NL), out_shape=(jax.ShapeDty...  68.2 us
    unnamed x12, local copies, waits for them, and re-layouts  5.71 us

commit v1 on v0

--- a/solution.py
+++ b/solution.py
@@ -24,6 +24,32 @@
 
 def dot(a, b):
     return jnp.dot(a, b, precision=lax.Precision.HIGHEST, preferred_element_type=F32)
+
+
+def split(x, terms):
+    parts = []
+    for _ in range(terms):
+        part = x.astype(jnp.bfloat16)
+        parts.append(part)
+        x = x - part.astype(F32)
+    return parts
+
+
+def picked(x, selector):
+    selector = selector.astype(jnp.bfloat16)
+    high, middle, low = [jnp.dot(part, selector, preferred_element_type=F32) for part in split(x, 3)]
+    return high + (middle + low)
+
+
+def mixed(matrix, x):
+    high, low = split(matrix, 2)
+    x_high, x_low = split(x, 2)
+    product = lambda a, b: jnp.dot(a, b, preferred_element_type=F32)
+    return product(high, x_high) + (product(high, x_low) + product(low, x_high))
+
+
+def widened(x, width):
+    return x if width == x.shape[1] else jnp.concatenate([x] * (width // x.shape[1]), axis=1)
 
 
 def rolled(x, shift):
@@ -61,12 +87,17 @@
     return out
 
 
-def kernel(NT, NL, starts, coarse_old, mean_depth, coupling, wet_cells, ends, coarse_new,
-           YA, Y1, Y2, PB, WET, WX, HB, KF, KC, WW, W2, WR, WP, DL, TX, RX, TC, RC, CT, PC, WC, RES,
+def kernel(NT, NL, starts_in, old_in, depth_in, coupling_in, wet_in, ends, coarse_new,
+           SV, OV, CV, WV, DS, DP, CF, in_sem, YA, Y1, Y2, PB, WET, WX, HB, KF, KC, WW, W2, WR, WP, DL, TX, RX, TC, RC, CT, PC, WC, RES,
            CO, BW, CN, C0, P0, W0,
            hs_send, hs_recv, wx_send, wx_recv, tx_send, rx_recv, tc_send, rc_recv):
+    starts, coarse_old, mean_depth, coupling, wet_cells = SV, OV, DS, CV, WV
     R, W = wet_cells.shape
     L = 8
+    fetches = [pltpu.make_async_copy(source, target, in_sem.at[i]) for i, (source, target) in enumerate(
+        ((starts_in, SV), (wet_in, WV), (coupling_in, CV), (depth_in, DS), (old_in, OV)))]
+    for fetch in fetches:
+        fetch.start()
     RC_ROWS, WCO = R // 2, W // 2
     SLAB = WCO // NT
     n, q = lax.axis_index("tm"), lax.axis_index("lat")
@@ -86,24 +117,26 @@
             for j in range(NT):
                 greet(lax.rem(n + j, NT), q + d)
 
+    fetches[0].wait()
     for f in range(3):
         for b in range(R // 8):
             YA[pl.ds(HALO + 8 * b, 8), f] = jnp.swapaxes(starts[f, :, pl.ds(8 * b, 8), :], 0, 1)
 
     pl.semaphore_wait(barrier, (NT - 1) + NT * up.astype(jnp.int32) + NT * down.astype(jnp.int32))
 
-    def halo_copy(k, side):
-        first = HALO if side == -1 else R
+    def halo_copy(k, side, j):
+        row = HALO + HALO - 1 - j if side == -1 else R + j
         slot = 1 if side == -1 else 0
         return pltpu.make_async_remote_copy(
-            src_ref=YA.at[pl.ds(first, HALO)], dst_ref=HB.at[k, slot],
-            send_sem=hs_send.at[k, slot], recv_sem=hs_recv.at[k, slot],
+            src_ref=YA.at[row], dst_ref=HB.at[k, slot, row - HALO if side == -1 else j],
+            send_sem=hs_send.at[k, slot, j], recv_sem=hs_recv.at[k, slot, j],
             device_id=(n, q + side), device_id_type=MESH)
 
-    def halo_arrival(k, slot, side):
-        return pltpu.make_async_remote_copy(
-            src_ref=YA.at[pl.ds(0, HALO)], dst_ref=HB.at[k, slot],
-            send_sem=hs_send.at[k, slot], recv_sem=hs_recv.at[k, slot],
+    def halo_arrival(k, side, j):
+        slot = 0 if side == -1 else 1
+        return pltpu.make_async_remote_copy(
+            src_ref=YA.at[0], dst_ref=HB.at[k, slot, j if side == -1 else HALO - 1 - j],
+            send_sem=hs_send.at[k, slot, j], recv_sem=hs_recv.at[k, slot, j],
             device_id=(n, q + side), device_id_type=MESH)
 
     def wet_copy(side):
@@ -112,13 +145,16 @@
             src_ref=wet_cells, dst_ref=WX.at[slot], send_sem=wx_send.at[slot], recv_sem=wx_recv.at[slot],
             device_id=(n, q + side), device_id_type=MESH)
 
-    def send_halos(k):
+    def send_row(k, j):
         for side in (-1, 1):
             @pl.when(inside_side[side])
             def _(side=side):
-                halo_copy(k, side).start()
-
-    send_halos(0)
+                halo_copy(k, side, j).start()
+
+    for j in range(HALO):
+        send_row(0, j)
+    for fetch in fetches[1:]:
+        fetch.wait()
     for side in (-1, 1):
         @pl.when(inside_side[side])
         def _(side=side):
@@ -139,28 +175,36 @@
     blocks = jnp.where(iota((KN, KN), 0) // L == iota((KN, KN), 1) // L, blocks, 0.0)
     KF[...] = 0.5 * blocks
     KC[...] = 0.25 * blocks
+    for shift in range(L):
+        column = (iota((L, L), 0) - shift + L) & (L - 1)
+        part = jnp.sum(jnp.where(iota((L, L), 1) == column, coupling[...], 0.0), axis=1, keepdims=True)
+        CF[shift] = jnp.broadcast_to(0.5 * part, (L, 128))
+
+    layer = iota((L, 128), 0)
+    value = jnp.zeros((L, 128), F32)
+    for l in range(L):
+        value = jnp.where(layer == l, mean_depth[l], value)
+    DP[...] = value
 
     def depth_of(width):
-        rows = iota((L, width), 0)
-        value = jnp.zeros((L, width), F32)
-        for l in range(L):
-            value = jnp.where(rows == l, mean_depth[l], value)
-        return value
+        return widened(DP[...], width)
 
     wet_own = wet_cells[...].astype(F32)
     for r in range(R):
         WET[HALO + r] = jnp.broadcast_to(wet_own[r:r + 1, :], (L, W))
 
-    target = (iota((W, W), 1) // 64 * SLAB - 16 + iota((W, W), 1) % 64 + WCO) % WCO
-    WW[...] = (iota((W, W), 0) // 2 == target).astype(F32)
-    W2[...] = (iota((WCO, W), 0) == target[:WCO]).astype(F32)
-    WR[...] = (iota((W, WCO), 0) // 2 == iota((W, WCO), 1)).astype(F32)
-    WP[...] = (iota((WCO, W), 1) // 2 == iota((WCO, W), 0)).astype(F32)
+    position = iota((8, W), 1)
+    target = ((position >> 6) * SLAB - 16 + (position & 63)) & (WCO - 1)
+    target = target[:1]
+    WW[...] = ((iota((W, W), 0) >> 1) == target).astype(F32)
+    W2[...] = (iota((WCO, W), 0) == target).astype(F32)
+    WR[...] = ((iota((W, WCO), 0) >> 1) == iota((W, WCO), 1)).astype(F32)
+    WP[...] = ((iota((WCO, W), 1) >> 1) == iota((WCO, W), 0)).astype(F32)
 
     @pl.when(n == 0)
     def _():
         sums = jnp.stack([YA[HALO + 2 * i] + YA[HALO + 1 + 2 * i] for i in range(RC_ROWS)])
-        C0[pl.ds(1, RC_ROWS)] = (0.25 * dot(sums.reshape(-1, W), WR[...])).reshape(RC_ROWS, 3, L, WCO)
+        C0[pl.ds(1, RC_ROWS)] = (0.25 * picked(sums.reshape(-1, W), WR[...])).reshape(RC_ROWS, 3, L, WCO)
 
     for f in range(3):
         CO[:, f] = jnp.swapaxes(coarse_old[f], 0, 1)
@@ -181,11 +225,18 @@
         rows = [src[pl.ds(a, c), 0] for a, c in pieces]
         rows = rows[0] if len(rows) == 1 else jnp.concatenate(rows, axis=0)
         size = count * L
-        result = dot(KF[pl.ds(0, size), pl.ds(0, size)], rows.reshape(size, W)).reshape(count, L, W)
+        result = mixed(KF[pl.ds(0, size), pl.ds(0, size)], rows.reshape(size, W)).reshape(count, L, W)
         at = 0
         for a, c in pieces:
             PB[stage, pl.ds(a, c)] = result[at:at + c]
             at += c
+
+    def row_pressure(stage, r):
+        e = stages[stage][0][r, 0]
+        total = widened(CF[0], W) * e
+        for shift in range(1, L):
+            total = total + widened(CF[shift], W) * pltpu.roll(e, shift, axis=0)
+        PB[stage, r] = total
 
     def fine_row(stage, r):
         src, dst, weights, g = stages[stage]
@@ -196,13 +247,13 @@
 
     def coarse_first():
         sums = jnp.stack([YA[1] + YA[2], YA[HALO + R] + YA[HALO + R + 1]])
-        outer = (0.25 * dot(sums.reshape(-1, W), WR[...])).reshape(2, 3, L, WCO)
+        outer = (0.25 * picked(sums.reshape(-1, W), WR[...])).reshape(2, 3, L, WCO)
         C0[0] = outer[0]
         C0[RC_ROWS + 1] = outer[1]
         size = (RC_ROWS + 2) * L
-        P0[...] = dot(KC[pl.ds(0, size), pl.ds(0, size)], C0[:, 0].reshape(size, WCO)).reshape(RC_ROWS + 2, L, WCO)
+        P0[...] = mixed(KC[pl.ds(0, size), pl.ds(0, size)], C0[:, 0].reshape(size, WCO)).reshape(RC_ROWS + 2, L, WCO)
         pairs = (iota((RC_ROWS, R), 1) // 2 == iota((RC_ROWS, R), 0)).astype(F32)
-        wet_full = (dot(dot(pairs, wet_cells[...].astype(F32)), WR[...]) > 3.5).astype(F32)
+        wet_full = (jnp.dot(jnp.dot(pairs, wet_cells[...].astype(F32)), WR[...]) > 3.5).astype(F32)
         for i in range(RC_ROWS):
             W0[i] = jnp.broadcast_to(wet_full[i:i + 1, :], (L, WCO))
 
@@ -214,6 +265,60 @@
             for i in range(3):
                 CN[r - 1, i] = new[i]
 
+    HU = RC_ROWS // 2
+    lanes = iota((L, 128), 1)
+
+    def slot_of(unit):
+        return {1: 0, 2: 1, 0: 2, 3: 3}[unit]
+
+    def deltas(first, last):
+        rows = range(2 * first, 2 * last)
+        count = len(rows)
+        sums = jnp.stack([YA[HALO + 2 * i] + YA[HALO + 1 + 2 * i] for i in rows])
+        bias = BW[pl.ds(2 * first * 3 * L, count * 3 * L)]
+        DL[pl.ds(2 * first, count)] = (0.25 * picked(sums.reshape(-1, W), WW[...]) + bias).reshape(count, 3, L, W)
+        for i in range(first, last):
+            for f in range(3):
+                for j in range(NT // 2):
+                    a = DL[2 * i, f, :, pl.ds(128 * j, 128)]
+                    b = DL[2 * i + 1, f, :, pl.ds(128 * j, 128)]
+                    TX[2 * j, slot_of(i), f] = jnp.where(lanes < 64, a, rolled(b, 64))
+                    TX[2 * j + 1, slot_of(i), f] = jnp.where(lanes < 64, rolled(a, 64), b)
+
+    def piece(d, phase, units):
+        if d == 0 or units == 4:
+            return 2 * phase, 2
+        if phase == 1:
+            return (3 if d == 1 else 2), 1
+        return {1: (0, 0), 2: (1 if d == 1 else 0, 1), 3: (0, 2)}[units]
+
+    def delta_copy(m, d, phase, units):
+        first, count = piece(d, phase, units)
+        return pltpu.make_async_remote_copy(
+            src_ref=TX.at[m, pl.ds(first, count)], dst_ref=RX.at[n, pl.ds(HU * (1 - d) + first, count)],
+            send_sem=tx_send.at[m, d + 1, phase], recv_sem=rx_recv.at[n, d + 1, phase],
+            device_id=(m, q + d), device_id_type=MESH)
+
+    def delta_arrival(s, d, phase, units):
+        first, count = piece(d, phase, units)
+        return pltpu.make_async_remote_copy(
+            src_ref=TX.at[0, pl.ds(first, count)], dst_ref=RX.at[s, pl.ds(HU * (1 - d) + first, count)],
+            send_sem=tx_send.at[0, d + 1, phase], recv_sem=rx_recv.at[s, d + 1, phase],
+            device_id=(s, q - d), device_id_type=MESH)
+
+    def for_deltas(phase, act):
+        for units in sorted({(NT - s) // 2 for s in range(NT - 1)}):
+            @pl.when((n < NT - 1) & ((NT - n) // 2 == units))
+            def _(units=units):
+                @pl.loop(0, NT)
+                def _(j):
+                    m = lax.rem(n + j, NT)
+                    for d, there in ((1, down), (-1, up), (0, j > 0)):
+                        if piece(d, phase, units)[1]:
+                            @pl.when(there)
+                            def _(d=d):
+                                act(delta_copy(m, d, phase, units))
+
     @pl.loop(0, STEPS)
     def _(k):
         for stage in range(3):
@@ -224,14 +329,21 @@
                 for more in range(2):
                     fine_row(stage, HALO + stage + 1 + 2 * j + more)
 
+        @pl.when(k == STEPS - 1)
+        def _():
+            deltas(1, 3)
+            for_deltas(0, lambda copy: copy.start())
+
         for side in (-1, 1):
             slot = 0 if side == -1 else 1
 
             @pl.when(inside_side[side])
             def _(side=side, slot=slot):
-                halo_arrival(k, slot, side).wait_recv()
+                for j in range(HALO):
+                    halo_arrival(k, side, j).wait_recv()
                 YA[pl.ds(0 if side == -1 else HALO + R, HALO)] = HB[k, slot]
-                halo_copy(k, side).wait_send()
+                for j in range(HALO):
+                    halo_copy(k, side, j).wait_send()
 
         @pl.when(k == 0)
         def _():
@@ -244,75 +356,32 @@
                 WET[r] = jnp.broadcast_to(WX[0, R - HALO + r:R - HALO + r + 1, :].astype(F32), (L, W))
                 WET[HALO + R + r] = jnp.broadcast_to(WX[1, r:r + 1, :].astype(F32), (L, W))
 
+        for j in range(HALO):
+            for stage in range(3):
+                low, high = HALO - j + stage, HALO + R - 1 + j - stage
+                row_pressure(stage, low - 1)
+                row_pressure(stage, high + 1)
+                fine_row(stage, low)
+                fine_row(stage, high)
+
+            @pl.when(k < STEPS - 1)
+            def _(j=j):
+                send_row(k + 1, j)
+
+        @pl.when(k == 0)
+        def _():
             @pl.when(n == 0)
             def _():
                 coarse_first()
-                BW[...] = dot((CN[...] - CO[...]).reshape(-1, WCO), W2[...])
+                BW[...] = picked((CN[...] - CO[...]).reshape(-1, WCO), W2[...])
 
             @pl.when(n > 0)
             def _():
-                BW[...] = dot((-CO[...]).reshape(-1, WCO), W2[...])
-
-        for stage in range(3):
-            pressure(stage, [(stage, HALO), (HALO + R - stage, HALO)])
-
-            @pl.loop(0, HALO)
-            def _(j, stage=stage):
-                fine_row(stage, stage + 1 + j)
-                fine_row(stage, R - stage + 2 + j)
-
-        @pl.when(k < STEPS - 1)
-        def _():
-            send_halos(k + 1)
-
-    sums = jnp.stack([YA[HALO + 2 * i] + YA[HALO + 1 + 2 * i] for i in range(RC_ROWS)])
-    DL[...] = (0.25 * dot(sums.reshape(-1, W), WW[...]) + BW[...]).reshape(RC_ROWS, 3, L, W)
-    lanes = iota((L, 128), 1)
-    for i in range(RC_ROWS // 2):
-        for f in range(3):
-            for j in range(NT // 2):
-                a = DL[2 * i, f, :, pl.ds(128 * j, 128)]
-                b = DL[2 * i + 1, f, :, pl.ds(128 * j, 128)]
-                TX[2 * j, i, f] = jnp.where(lanes < 64, a, rolled(b, 64))
-                TX[2 * j + 1, i, f] = jnp.where(lanes < 64, rolled(a, 64), b)
-
-    HU = RC_ROWS // 2
-
-    def delta_copy(m, d, units):
-        first, to = {0: (0, HU), 1: (HU - units, HU - units), -1: (0, 2 * HU)}[d]
-        return pltpu.make_async_remote_copy(
-            src_ref=TX.at[m, pl.ds(first, units)], dst_ref=RX.at[n, pl.ds(to, units)],
-            send_sem=tx_send.at[m, d + 1], recv_sem=rx_recv.at[n, d + 1],
-            device_id=(m, q + d), device_id_type=MESH)
-
-    def delta_arrival(s, d, units):
-        to = {0: HU, 1: HU - units, -1: 2 * HU}[d]
-        return pltpu.make_async_remote_copy(
-            src_ref=TX.at[0, pl.ds(0, units)], dst_ref=RX.at[s, pl.ds(to, units)],
-            send_sem=tx_send.at[0, d + 1], recv_sem=rx_recv.at[s, d + 1],
-            device_id=(s, q - d), device_id_type=MESH)
-
-    def for_deltas(act):
-        for units in sorted({(NT - s) // 2 for s in range(NT - 1)}):
-            @pl.when((n < NT - 1) & ((NT - n) // 2 == units))
-            def _(units=units):
-                @pl.loop(0, NT)
-                def _(j):
-                    m = lax.rem(n + j, NT)
-
-                    @pl.when(down)
-                    def _():
-                        act(delta_copy(m, 1, units))
-
-                    @pl.when(up)
-                    def _():
-                        act(delta_copy(m, -1, units))
-
-                    @pl.when(j > 0)
-                    def _():
-                        act(delta_copy(m, 0, HU))
-
-    for_deltas(lambda copy: copy.start())
+                BW[...] = picked((-CO[...]).reshape(-1, WCO), W2[...])
+
+    deltas(0, 1)
+    deltas(3, 4)
+    for_deltas(1, lambda copy: copy.start())
 
     @pl.when(n < NT - 1)
     def _():
@@ -320,31 +389,25 @@
 
     E = 3 * RC_ROWS
     col = iota((W, 128), 1)
-    own = (n * SLAB - 16 + col + WCO) % WCO
-    picks = jnp.where((iota((W, 128), 0) // 2 == own) & (col < 64), 1.0, 0.0).astype(F32)
+    own = (n * SLAB - 16 + col) & (WCO - 1)
+    picks = jnp.where(((iota((W, 128), 0) >> 1) == own) & (col < 64), 1.0, 0.0).astype(F32)
     pairs = (iota((RC_ROWS, R), 1) // 2 == iota((RC_ROWS, R), 0)).astype(F32)
     for part, cells in enumerate((WX[0], wet_cells[...], WX[1])):
-        window = (dot(dot(pairs, cells.astype(F32)), picks) > 3.5).astype(F32)
+        window = (jnp.dot(jnp.dot(pairs, cells.astype(F32)), picks) > 3.5).astype(F32)
         for i in range(RC_ROWS):
             WC[part * RC_ROWS + i] = jnp.broadcast_to(window[i:i + 1, :], (L, 128))
 
     def arrived(s):
-        h = (NT - s) // 2
-
-        @pl.when(up)
-        def _():
-            delta_arrival(s, 1, h).wait_recv()
-
-        @pl.when(down)
-        def _():
-            delta_arrival(s, -1, h).wait_recv()
-
-        @pl.when(n != s)
-        def _():
-            delta_arrival(s, 0, HU).wait_recv()
+        units = (NT - s) // 2
+        for phase in range(2):
+            for d, there in ((1, up), (-1, down), (0, n != s)):
+                if piece(d, phase, units)[1]:
+                    @pl.when(there)
+                    def _(d=d, phase=phase):
+                        delta_arrival(s, d, phase, units).wait_recv()
 
     def row_of(s, r, f):
-        x = RX[s, r // 2, f]
+        x = RX[s, r // 2 // HU * HU + slot_of(r // 2 % HU), f]
         return x if r % 2 == 0 else rolled(x, 64)
 
     arrived(0)
@@ -369,7 +432,7 @@
         h = NT - 1 - s
         lo, hi = RC_ROWS - h, 2 * RC_ROWS + h
         size = (hi - lo + 2) * L
-        PC[pl.ds(lo - 1, hi - lo + 2)] = dot(
+        PC[pl.ds(lo - 1, hi - lo + 2)] = mixed(
             KC[pl.ds(0, size), pl.ds(0, size)], now[pl.ds(lo - 1, hi - lo + 2), 0].reshape(size, 128)
         ).reshape(hi - lo + 2, L, 128)
         if s < NT - 1:
@@ -414,7 +477,7 @@
                         value = jnp.where(group == m, rolled(RC[4 * j + m, b, i], SLAB * (m - g)), value)
                     CN[r, i, :, pl.ds(128 * j, 128)] = value
 
-    change = dot((CN[...] - CO[...]).reshape(-1, WCO), WP[...]).reshape(RC_ROWS, 3, L, W)
+    change = picked((CN[...] - CO[...]).reshape(-1, WCO), WP[...]).reshape(RC_ROWS, 3, L, W)
     for i in range(3):
         coarse_new[i] = jnp.swapaxes(CN[:, i], 0, 1)
     for r in range(RC_ROWS):
@@ -425,7 +488,8 @@
         for b in range(R // 8):
             ends[i, :, pl.ds(8 * b, 8), :] = jnp.swapaxes(YA[pl.ds(HALO + 8 * b, 8), i], 0, 1)
 
-    for_deltas(lambda copy: copy.wait_send())
+    for phase in range(2):
+        for_deltas(phase, lambda copy: copy.wait_send())
     for s in range(1, NT):
         @pl.when(n != s)
         def _(s=s):
@@ -440,12 +504,15 @@
     vmem = lambda *shape: pltpu.VMEM(shape, F32)
     sems = lambda *shape: pltpu.SemaphoreType.DMA(shape)
     space = pl.BlockSpec(memory_space=pltpu.VMEM)
+    far = pl.BlockSpec(memory_space=pltpu.HBM)
     ends, coarse_new = pl.pallas_call(
         functools.partial(kernel, NT, NL),
         out_shape=(jax.ShapeDtypeStruct((3, L, R, W), F32), jax.ShapeDtypeStruct((3, L, C, WCO), F32)),
-        in_specs=[space, space, pl.BlockSpec(memory_space=pltpu.SMEM), space, space],
+        in_specs=[far] * 5,
         out_specs=(space, space),
         scratch_shapes=[
+            vmem(3, L, R, W), vmem(3, L, C, WCO), vmem(L, L), pltpu.VMEM((R, W), jnp.int32), pltpu.SMEM((L,), F32),
+            vmem(L, 128), vmem(L, L, 128), sems(5),
             vmem(E, 3, L, W), vmem(E, 3, L, W), vmem(E, 3, L, W), vmem(3, E, L, W), vmem(E, L, W),
             pltpu.VMEM((2, R, W), jnp.int32), vmem(STEPS, 2, HALO, 3, L, W),
             vmem(3 * C * L, 3 * C * L), vmem(3 * C * L, 3 * C * L),
@@ -455,10 +522,10 @@
             vmem(2, 3 * C, 3, L, 128), vmem(3 * C, L, 128), vmem(3 * C, L, 128), vmem(C, 3, L, 128),
             vmem(C, 3, L, WCO), vmem(C * 3 * L, W), vmem(C, 3, L, WCO),
             vmem(C + 2, 3, L, WCO), vmem(C + 2, L, WCO), vmem(C, L, WCO),
-            sems(STEPS, 2), sems(STEPS, 2), sems(2), sems(2), sems(NT, 3), sems(NT - 1, 3), sems(NT), sems(NT),
+            sems(STEPS, 2, HALO), sems(STEPS, 2, HALO), sems(2), sems(2), sems(NT, 3, 2), sems(NT - 1, 3, 2), sems(NT), sems(NT),
         ],
         compiler_params=pltpu.CompilerParams(
-            collective_id=0, has_side_effects=True, vmem_limit_bytes=48 * 1024 * 1024),
+            collective_id=0, has_side_effects=True, vmem_limit_bytes=63 * 1024 * 1024),
     )(starts[0], coarse_old[0], mean_depth, coupling, wet_cells)
     return ends[None], coarse_new[None]
 

time: 74.8 us -> 62.3 us (0.83)
  Pallas kernels: 68.2 us -> 58.7 us
  local copies, waits for them, and re-layouts: 5.71 us -> 2.81 us
    pallas_call x1, Pallas kernels: 68.2 us -> 58.7 us  [local(): pl.pallas_call(functools.partial(kernel, NT, NL), out_shape=(jax.ShapeDty...]
    unnamed x12 -> x4, local copies, waits for them, and re-layouts: 5.71 us -> 2.81 us
where the time goes in v1:
time: 62.3 us; the launch traced here: 62.1 us
  Pallas kernels  58.7 us (94%)
  local copies, waits for them, and re-layouts  2.81 us (5%)
  between operations  0.65 us (1%)
    pallas_call x1, Pallas kernels, local(): pl.pallas_call(functools.partial(kernel, NT, NL), out_shape=(jax.ShapeDty...  58.7 us
    unnamed x4, local copies, waits for them, and re-layouts  2.81 us

profile of v1, /device:TPU:30, one launch (start us, length us, event | category | flops | bytes accessed | tf_op | source)
XLA Modules:
  0.0 62.1 jit_solution(12876878108837648791)
XLA Ops:
  0.6 58.7 %shard_map.68 = (f32[3,8,16,512]{3,2,1,0:T(8,128)}, f32[3,8,8,256]{3,2,1,0:T(8,128)}) custom-call(f32[3,8,16,512]{3,2,1,0:T(8,128)} %bitcast.4, f32[3,8,8,256]{3,2,1,0:T(8,128)} %bitcast.6, f32[8]{0:T(128)} %depth_in.1, f32[8,8]{1,0:T(8,128)} %coupling_in.1, s32[16,512]{1,0:T(8,128)} %wet_in.1), custom_call_target="tpu_custom_call" | custom-call | tf_op jit(solution)/shard_map/pallas_call | solution.py:508
  59.3 0.0 copy-start
  59.3 2.1 %copy.9 = f32[1,3,8,16,512]{4,3,2,1,0:T(8,128)} copy(f32[1,3,8,16,512]{4,3,2,1,0:T(8,128)} %bitcast.5) | data formatting | bytes 1572864
  61.5 0.0 copy-done
  61.5 0.7 %copy.10 = f32[1,3,8,8,256]{4,3,2,1,0:T(8,128)} copy(f32[1,3,8,8,256]{4,3,2,1,0:T(8,128)S(1)} %bitcast.7) | data formatting | bytes 393216
Async XLA Ops:
  59.3 2.1 %copy-start = (f32[3,8,8,256]{3,2,1,0:T(8,128)S(1)}, f32[3,8,8,256]{3,2,1,0:T(8,128)}, u32[]{:S(2)}) copy-start(f32[3,8,8,256]{3,2,1,0:T(8,128)} %get-tuple-element.5) | copy-start | bytes 589828

commit v2 on v1

--- a/solution.py
+++ b/solution.py
@@ -36,9 +36,9 @@
 
 
 def picked(x, selector):
-    selector = selector.astype(jnp.bfloat16)
-    high, middle, low = [jnp.dot(part, selector, preferred_element_type=F32) for part in split(x, 3)]
-    return high + (middle + low)
+    rows = x.shape[0]
+    result = jnp.dot(jnp.concatenate(split(x, 3), axis=0), selector, preferred_element_type=F32)
+    return result[:rows] + (result[rows:2 * rows] + result[2 * rows:])
 
 
 def mixed(matrix, x):
@@ -88,14 +88,14 @@
 
 
 def kernel(NT, NL, starts_in, old_in, depth_in, coupling_in, wet_in, ends, coarse_new,
-           SV, OV, CV, WV, DS, DP, CF, in_sem, YA, Y1, Y2, PB, WET, WX, HB, KF, KC, WW, W2, WR, WP, DL, TX, RX, TC, RC, CT, PC, WC, RES,
+           SV, OV, CV, WV, DS, DP, CF, in_sem, YA, Y1, Y2, PB, WET, WX, HB, KF, KC, WW, W2, WR, DL, TX, RX, TC, RC, CT, PC, WC, RES,
            CO, BW, CN, C0, P0, W0,
-           hs_send, hs_recv, wx_send, wx_recv, tx_send, rx_recv, tc_send, rc_recv):
+           hs_send, hs_recv, wx_send, wx_recv, tx_send, rx_recv, fw_send, fw_recv, tc_send, rc_recv):
     starts, coarse_old, mean_depth, coupling, wet_cells = SV, OV, DS, CV, WV
     R, W = wet_cells.shape
     L = 8
     fetches = [pltpu.make_async_copy(source, target, in_sem.at[i]) for i, (source, target) in enumerate(
-        ((starts_in, SV), (wet_in, WV), (coupling_in, CV), (depth_in, DS), (old_in, OV)))]
+        [(starts_in.at[f], SV.at[f]) for f in range(3)] + [(wet_in, WV), (coupling_in, CV), (depth_in, DS), (old_in, OV)])]
     for fetch in fetches:
         fetch.start()
     RC_ROWS, WCO = R // 2, W // 2
@@ -114,15 +114,14 @@
     for d in (-1, 1):
         @pl.when(inside_side[d])
         def _(d=d):
-            for j in range(NT):
-                greet(lax.rem(n + j, NT), q + d)
-
-    fetches[0].wait()
+            greet(n, q + d)
+
     for f in range(3):
+        fetches[f].wait()
         for b in range(R // 8):
             YA[pl.ds(HALO + 8 * b, 8), f] = jnp.swapaxes(starts[f, :, pl.ds(8 * b, 8), :], 0, 1)
 
-    pl.semaphore_wait(barrier, (NT - 1) + NT * up.astype(jnp.int32) + NT * down.astype(jnp.int32))
+    pl.semaphore_wait(barrier, (NT - 1) + up.astype(jnp.int32) + down.astype(jnp.int32))
 
     def halo_copy(k, side, j):
         row = HALO + HALO - 1 - j if side == -1 else R + j
@@ -153,7 +152,7 @@
 
     for j in range(HALO):
         send_row(0, j)
-    for fetch in fetches[1:]:
+    for fetch in fetches[3:]:
         fetch.wait()
     for side in (-1, 1):
         @pl.when(inside_side[side])
@@ -196,10 +195,10 @@
     position = iota((8, W), 1)
     target = ((position >> 6) * SLAB - 16 + (position & 63)) & (WCO - 1)
     target = target[:1]
-    WW[...] = ((iota((W, W), 0) >> 1) == target).astype(F32)
-    W2[...] = (iota((WCO, W), 0) == target).astype(F32)
-    WR[...] = ((iota((W, WCO), 0) >> 1) == iota((W, WCO), 1)).astype(F32)
-    WP[...] = ((iota((WCO, W), 1) >> 1) == iota((WCO, W), 0)).astype(F32)
+    selector = lambda where: jnp.where(where, 1.0, 0.0).astype(jnp.bfloat16)
+    WW[...] = selector((iota((W, W), 0) >> 1) == target)
+    W2[...] = selector(iota((WCO, W), 0) == target)
+    WR[...] = selector((iota((W, WCO), 0) >> 1) == iota((W, WCO), 1))
 
     @pl.when(n == 0)
     def _():
@@ -253,7 +252,7 @@
         size = (RC_ROWS + 2) * L
         P0[...] = mixed(KC[pl.ds(0, size), pl.ds(0, size)], C0[:, 0].reshape(size, WCO)).reshape(RC_ROWS + 2, L, WCO)
         pairs = (iota((RC_ROWS, R), 1) // 2 == iota((RC_ROWS, R), 0)).astype(F32)
-        wet_full = (jnp.dot(jnp.dot(pairs, wet_cells[...].astype(F32)), WR[...]) > 3.5).astype(F32)
+        wet_full = (jnp.dot(jnp.dot(pairs, wet_cells[...].astype(F32)), WR[...].astype(F32)) > 3.5).astype(F32)
         for i in range(RC_ROWS):
             W0[i] = jnp.broadcast_to(wet_full[i:i + 1, :], (L, WCO))
 
@@ -271,13 +270,13 @@
     def slot_of(unit):
         return {1: 0, 2: 1, 0: 2, 3: 3}[unit]
 
-    def deltas(first, last):
-        rows = range(2 * first, 2 * last)
-        count = len(rows)
+    def deltas(units):
+        rows = [2 * unit + more for unit in units for more in range(2)]
         sums = jnp.stack([YA[HALO + 2 * i] + YA[HALO + 1 + 2 * i] for i in rows])
-        bias = BW[pl.ds(2 * first * 3 * L, count * 3 * L)]
-        DL[pl.ds(2 * first, count)] = (0.25 * picked(sums.reshape(-1, W), WW[...]) + bias).reshape(count, 3, L, W)
-        for i in range(first, last):
+        change = (0.25 * picked(sums.reshape(-1, W), WW[...])).reshape(len(rows), 3, L, W)
+        for at, i in enumerate(rows):
+            DL[i] = change[at] + BW[pl.ds(i * 3 * L, 3 * L)].reshape(3, L, W)
+        for i in units:
             for f in range(3):
                 for j in range(NT // 2):
                     a = DL[2 * i, f, :, pl.ds(128 * j, 128)]
@@ -292,47 +291,67 @@
             return (3 if d == 1 else 2), 1
         return {1: (0, 0), 2: (1 if d == 1 else 0, 1), 3: (0, 2)}[units]
 
-    def delta_copy(m, d, phase, units):
-        first, count = piece(d, phase, units)
-        return pltpu.make_async_remote_copy(
-            src_ref=TX.at[m, pl.ds(first, count)], dst_ref=RX.at[n, pl.ds(HU * (1 - d) + first, count)],
-            send_sem=tx_send.at[m, d + 1, phase], recv_sem=rx_recv.at[n, d + 1, phase],
-            device_id=(m, q + d), device_id_type=MESH)
-
-    def delta_arrival(s, d, phase, units):
-        first, count = piece(d, phase, units)
-        return pltpu.make_async_remote_copy(
-            src_ref=TX.at[0, pl.ds(first, count)], dst_ref=RX.at[s, pl.ds(HU * (1 - d) + first, count)],
-            send_sem=tx_send.at[0, d + 1, phase], recv_sem=rx_recv.at[s, d + 1, phase],
-            device_id=(s, q - d), device_id_type=MESH)
+    def delta_copy(m, phase):
+        return pltpu.make_async_remote_copy(
+            src_ref=TX.at[m, pl.ds(2 * phase, 2)], dst_ref=RX.at[n, pl.ds(HU + 2 * phase, 2)],
+            send_sem=tx_send.at[m, phase], recv_sem=rx_recv.at[n, phase],
+            device_id=(m, q), device_id_type=MESH)
+
+    def delta_arrival(s, phase):
+        return pltpu.make_async_remote_copy(
+            src_ref=TX.at[0, pl.ds(0, 2)], dst_ref=RX.at[s, pl.ds(HU + 2 * phase, 2)],
+            send_sem=tx_send.at[0, phase], recv_sem=rx_recv.at[s, phase],
+            device_id=(s, q), device_id_type=MESH)
 
     def for_deltas(phase, act):
-        for units in sorted({(NT - s) // 2 for s in range(NT - 1)}):
-            @pl.when((n < NT - 1) & ((NT - n) // 2 == units))
-            def _(units=units):
-                @pl.loop(0, NT)
-                def _(j):
-                    m = lax.rem(n + j, NT)
-                    for d, there in ((1, down), (-1, up), (0, j > 0)):
-                        if piece(d, phase, units)[1]:
-                            @pl.when(there)
-                            def _(d=d):
-                                act(delta_copy(m, d, phase, units))
+        @pl.when(n < NT - 1)
+        def _():
+            @pl.loop(1, NT)
+            def _(j):
+                act(delta_copy(lax.rem(n + j, NT), phase))
+
+    def send_deltas(phase):
+        for_deltas(phase, lambda copy: copy.start())
+
+        @pl.when(n < NT - 1)
+        def _():
+            RX[n, pl.ds(HU + 2 * phase, 2)] = TX[n, pl.ds(2 * phase, 2)]
+
+    def passing(s, d, phase):
+        first, count = piece(d, phase, (NT - s) // 2)
+        side = 0 if d == 1 else 1
+        return pltpu.make_async_remote_copy(
+            src_ref=RX.at[s, pl.ds(HU + first, count)], dst_ref=RX.at[s, pl.ds(HU * (1 - d) + first, count)],
+            send_sem=fw_send.at[s, side, phase], recv_sem=fw_recv.at[s, side, phase],
+            device_id=(n, q + d), device_id_type=MESH)
+
+    def passed_on(phase):
+        return [(s, d, there) for s in range(NT - 1) for d, there in ((1, down), (-1, up))
+                if piece(d, phase, (NT - s) // 2)[1]]
+
+    def pass_deltas(phase):
+        for s in range(NT - 1):
+            @pl.when(n != s)
+            def _(s=s):
+                delta_arrival(s, phase).wait_recv()
+            for t, d, there in passed_on(phase):
+                if t == s:
+                    @pl.when(there)
+                    def _(s=s, d=d):
+                        passing(s, d, phase).start()
 
     @pl.loop(0, STEPS)
     def _(k):
         for stage in range(3):
             pressure(stage, [(HALO + stage, R - 2 * stage)])
 
-            @pl.loop(0, (R - 2 * (stage + 1)) // 2)
-            def _(j, stage=stage):
-                for more in range(2):
-                    fine_row(stage, HALO + stage + 1 + 2 * j + more)
+            for r in range(R - 2 * (stage + 1)):
+                fine_row(stage, HALO + stage + 1 + r)
 
         @pl.when(k == STEPS - 1)
         def _():
-            deltas(1, 3)
-            for_deltas(0, lambda copy: copy.start())
+            deltas((1, 2))
+            send_deltas(0)
 
         for side in (-1, 1):
             slot = 0 if side == -1 else 1
@@ -379,13 +398,11 @@
             def _():
                 BW[...] = picked((-CO[...]).reshape(-1, WCO), W2[...])
 
-    deltas(0, 1)
-    deltas(3, 4)
-    for_deltas(1, lambda copy: copy.start())
-
-    @pl.when(n < NT - 1)
-    def _():
-        RX[n, pl.ds(HU, HU)] = TX[n]
+    keep = pltpu.make_async_copy(YA.at[pl.ds(HALO, R)], ends, in_sem.at[5 + 2])
+    keep.start()
+    deltas((0, 3))
+    send_deltas(1)
+    pass_deltas(0)
 
     E = 3 * RC_ROWS
     col = iota((W, 128), 1)
@@ -397,14 +414,15 @@
         for i in range(RC_ROWS):
             WC[part * RC_ROWS + i] = jnp.broadcast_to(window[i:i + 1, :], (L, 128))
 
+    pass_deltas(1)
+
     def arrived(s):
-        units = (NT - s) // 2
         for phase in range(2):
-            for d, there in ((1, up), (-1, down), (0, n != s)):
-                if piece(d, phase, units)[1]:
-                    @pl.when(there)
+            for t, d, _ in passed_on(phase):
+                if t == s:
+                    @pl.when(up if d == 1 else down)
                     def _(d=d, phase=phase):
-                        delta_arrival(s, d, phase, units).wait_recv()
+                        passing(s, d, phase).wait_recv()
 
     def row_of(s, r, f):
         x = RX[s, r // 2 // HU * HU + slot_of(r // 2 % HU), f]
@@ -431,10 +449,12 @@
         now, later = CT.at[(s - 1) % 2], CT.at[s % 2]
         h = NT - 1 - s
         lo, hi = RC_ROWS - h, 2 * RC_ROWS + h
-        size = (hi - lo + 2) * L
-        PC[pl.ds(lo - 1, hi - lo + 2)] = mixed(
-            KC[pl.ds(0, size), pl.ds(0, size)], now[pl.ds(lo - 1, hi - lo + 2), 0].reshape(size, 128)
-        ).reshape(hi - lo + 2, L, 128)
+        for r in range(lo - 1, hi + 1):
+            e = now[r, 0]
+            total = (0.5 * CF[0]) * e
+            for shift in range(1, L):
+                total = total + (0.5 * CF[shift]) * pltpu.roll(e, shift, axis=0)
+            PC[r] = total
         if s < NT - 1:
             arrived(s)
         for r in range(lo, hi):
@@ -477,23 +497,35 @@
                         value = jnp.where(group == m, rolled(RC[4 * j + m, b, i], SLAB * (m - g)), value)
                     CN[r, i, :, pl.ds(128 * j, 128)] = value
 
-    change = picked((CN[...] - CO[...]).reshape(-1, WCO), WP[...]).reshape(RC_ROWS, 3, L, W)
-    for i in range(3):
-        coarse_new[i] = jnp.swapaxes(CN[:, i], 0, 1)
-    for r in range(RC_ROWS):
-        for i in range(3):
-            for more in range(2):
-                YA[HALO + 2 * r + more, i] = YA[HALO + 2 * r + more, i] + change[r, i]
-    for i in range(3):
-        for b in range(R // 8):
-            ends[i, :, pl.ds(8 * b, 8), :] = jnp.swapaxes(YA[pl.ds(HALO + 8 * b, 8), i], 0, 1)
-
+    coarse_new[...] = CN[...]
+    keep.wait()
     for phase in range(2):
         for_deltas(phase, lambda copy: copy.wait_send())
+        for s, d, there in passed_on(phase):
+            @pl.when(there)
+            def _(s=s, d=d, phase=phase):
+                passing(s, d, phase).wait_send()
     for s in range(1, NT):
         @pl.when(n != s)
         def _(s=s):
             result_copy(s).wait_send()
+
+
+def correct(state, coarse_new, coarse_old, ends, result, WP):
+    R, _, L, W = state.shape
+    C, WCO = R // 2, W // 2
+
+    @pl.when(pl.program_id(0) == 0)
+    def _():
+        WP[...] = jnp.where((iota((WCO, W), 1) >> 1) == iota((WCO, W), 0), 1.0, 0.0).astype(jnp.bfloat16)
+
+    new = coarse_new[:, 0]
+    result[0] = jnp.swapaxes(new, 0, 1)
+    change = new - jnp.swapaxes(coarse_old[0], 0, 1)
+    change = picked(change.reshape(C * L, WCO), WP[...]).reshape(C, L, W)
+    for b in range(R // 8):
+        rows = jnp.stack([state[8 * b + i, 0] + change[4 * b + i // 2] for i in range(8)])
+        ends[0, :, pl.ds(8 * b, 8), :] = jnp.swapaxes(rows, 0, 1)
 
 
 def local(NT, NL, starts, coarse_old, mean_depth, coupling, wet_cells):
@@ -502,32 +534,46 @@
     C, WCO = R // 2, W // 2
     E = R + 2 * HALO
     vmem = lambda *shape: pltpu.VMEM(shape, F32)
+    half = lambda *shape: pltpu.VMEM(shape, jnp.bfloat16)
     sems = lambda *shape: pltpu.SemaphoreType.DMA(shape)
     space = pl.BlockSpec(memory_space=pltpu.VMEM)
     far = pl.BlockSpec(memory_space=pltpu.HBM)
-    ends, coarse_new = pl.pallas_call(
+    state, coarse_new = pl.pallas_call(
         functools.partial(kernel, NT, NL),
-        out_shape=(jax.ShapeDtypeStruct((3, L, R, W), F32), jax.ShapeDtypeStruct((3, L, C, WCO), F32)),
+        out_shape=(jax.ShapeDtypeStruct((R, 3, L, W), F32), jax.ShapeDtypeStruct((C, 3, L, WCO), F32)),
         in_specs=[far] * 5,
-        out_specs=(space, space),
+        out_specs=(far, space),
         scratch_shapes=[
             vmem(3, L, R, W), vmem(3, L, C, WCO), vmem(L, L), pltpu.VMEM((R, W), jnp.int32), pltpu.SMEM((L,), F32),
-            vmem(L, 128), vmem(L, L, 128), sems(5),
+            vmem(L, 128), vmem(L, L, 128), sems(8),
             vmem(E, 3, L, W), vmem(E, 3, L, W), vmem(E, 3, L, W), vmem(3, E, L, W), vmem(E, L, W),
             pltpu.VMEM((2, R, W), jnp.int32), vmem(STEPS, 2, HALO, 3, L, W),
             vmem(3 * C * L, 3 * C * L), vmem(3 * C * L, 3 * C * L),
-            vmem(W, W), vmem(WCO, W), vmem(W, WCO), vmem(WCO, W), vmem(C, 3, L, W),
+            half(W, W), half(WCO, W), half(W, WCO), vmem(C, 3, L, W),
             vmem(NT, C // 2, 3, L, 128), vmem(NT - 1, 3 * C // 2, 3, L, 128),
             vmem(NT, 2, 3, L, 128), vmem(NT, 2, 3, L, 128),
             vmem(2, 3 * C, 3, L, 128), vmem(3 * C, L, 128), vmem(3 * C, L, 128), vmem(C, 3, L, 128),
             vmem(C, 3, L, WCO), vmem(C * 3 * L, W), vmem(C, 3, L, WCO),
             vmem(C + 2, 3, L, WCO), vmem(C + 2, L, WCO), vmem(C, L, WCO),
-            sems(STEPS, 2, HALO), sems(STEPS, 2, HALO), sems(2), sems(2), sems(NT, 3, 2), sems(NT - 1, 3, 2), sems(NT), sems(NT),
+            sems(STEPS, 2, HALO), sems(STEPS, 2, HALO), sems(2), sems(2), sems(NT, 2), sems(NT - 1, 2), sems(NT - 1, 2, 2), sems(NT - 1, 2, 2), sems(NT), sems(NT),
         ],
         compiler_params=pltpu.CompilerParams(
             collective_id=0, has_side_effects=True, vmem_limit_bytes=63 * 1024 * 1024),
     )(starts[0], coarse_old[0], mean_depth, coupling, wet_cells)
-    return ends[None], coarse_new[None]
+    ends, result = pl.pallas_call(
+        correct,
+        grid=(3,),
+        out_shape=(jax.ShapeDtypeStruct((3, L, R, W), F32), jax.ShapeDtypeStruct((3, L, C, WCO), F32)),
+        in_specs=[
+            pl.BlockSpec((R, 1, L, W), lambda f: (0, f, 0, 0)),
+            pl.BlockSpec((C, 1, L, WCO), lambda f: (0, f, 0, 0)),
+            pl.BlockSpec((1, L, C, WCO), lambda f: (f, 0, 0, 0)),
+        ],
+        out_specs=(pl.BlockSpec((1, L, R, W), lambda f: (f, 0, 0, 0)), pl.BlockSpec((1, L, C, WCO), lambda f: (f, 0, 0, 0))),
+        scratch_shapes=[pltpu.VMEM((WCO, W), jnp.bfloat16)],
+        compiler_params=pltpu.CompilerParams(vmem_limit_bytes=63 * 1024 * 1024),
+    )(state, coarse_new, coarse_old[0])
+    return ends[None], result[None]
 
 
 def solution(mesh):

time: 62.3 us -> 56.1 us (0.900)
  Pallas kernels: 58.7 us -> 55.3 us
  local copies, waits for them, and re-layouts: 2.81 us -> 0 us
    pallas_call x1, Pallas kernels: 58.7 us -> 51.9 us  [local(): pl.pallas_call(functools.partial(kernel, NT, NL), out_shape=(jax.ShapeDty...]
    pallas_call x0 -> x1, Pallas kernels: none -> 3.4 us  [local(): pl.pallas_call(correct, grid=(3,), out_shape=(jax.ShapeDtypeStruct((3, L,...]
    unnamed x4 -> x0, local copies, waits for them, and re-layouts: 2.81 us -> none
where the time goes in v2:
time: 56.1 us; the launch traced here: 56 us
  Pallas kernels  55.3 us (99%)
  between operations  0.64 us (1%)
    pallas_call x1, Pallas kernels, local(): pl.pallas_call(functools.partial(kernel, NT, NL), out_shape=(jax.ShapeDty...  51.9 us
    pallas_call x1, Pallas kernels, local(): pl.pallas_call(correct, grid=(3,), out_shape=(jax.ShapeDtypeStruct((3, L,...  3.4 us

profile of v2, /device:TPU:30, one launch (start us, length us, event | category | flops | bytes accessed | tf_op | source)
XLA Modules:
  0.0 56.0 jit_solution(8885949365702101012)
XLA Ops:
  0.6 51.9 %shard_map.68 = (f32[16,3,8,512]{3,2,1,0:T(8,128)}, f32[8,3,8,256]{3,2,1,0:T(8,128)}) custom-call(f32[3,8,16,512]{3,2,1,0:T(8,128)} %bitcast.6, f32[3,8,8,256]{3,2,1,0:T(8,128)} %bitcast.4, f32[8]{0:T(128)} %depth_in.1, f32[8,8]{1,0:T(8,128)} %coupling_in.1, s32[16,512]{1,0:T(8,128)} %wet_in.1), custom_call_target="tpu_custom_call" | custom-call | tf_op jit(solution)/shard_map/pallas_call | solution.py:541
  52.6 3.4 %shard_map.69 = (f32[3,8,16,512]{3,2,1,0:T(8,128)}, f32[3,8,8,256]{3,2,1,0:T(8,128)}) custom-call(f32[16,3,8,512]{3,2,1,0:T(8,128)} %get-tuple-element.6.state, f32[8,3,8,256]{3,2,1,0:T(8,128)} %get-tuple-element.7.coarse_new, f32[3,8,8,256]{3,2,1,0:T(8,128)} %bitcast.5), custom_call_target="tpu_custom_call" | custom-call | tf_op jit(solution)/shard_map/pallas_call | solution.py:563

commit v3 on v2

--- a/solution.py
+++ b/solution.py
@@ -116,12 +116,20 @@
         def _(d=d):
             greet(n, q + d)
 
+    pl.semaphore_wait(barrier, (NT - 1) + up.astype(jnp.int32) + down.astype(jnp.int32))
     for f in range(3):
         fetches[f].wait()
         for b in range(R // 8):
             YA[pl.ds(HALO + 8 * b, 8), f] = jnp.swapaxes(starts[f, :, pl.ds(8 * b, 8), :], 0, 1)
-
-    pl.semaphore_wait(barrier, (NT - 1) + up.astype(jnp.int32) + down.astype(jnp.int32))
+        for side in (-1, 1):
+            @pl.when(inside_side[side])
+            def _(f=f, side=side):
+                slot = 1 if side == -1 else 0
+                pltpu.make_async_remote_copy(
+                    src_ref=YA.at[pl.ds(HALO if side == -1 else R, HALO), f], dst_ref=HB.at[0, slot, :, f],
+                    send_sem=hs_send.at[0, slot, f], recv_sem=hs_recv.at[0, slot, f],
+                    device_id=(n, q + side), device_id_type=MESH).start()
+
 
     def halo_copy(k, side, j):
         row = HALO + HALO - 1 - j if side == -1 else R + j
@@ -150,8 +158,6 @@
             def _(side=side):
                 halo_copy(k, side, j).start()
 
-    for j in range(HALO):
-        send_row(0, j)
     for fetch in fetches[3:]:
         fetch.wait()
     for side in (-1, 1):
@@ -511,21 +517,33 @@
             result_copy(s).wait_send()
 
 
-def correct(state, coarse_new, coarse_old, ends, result, WP):
-    R, _, L, W = state.shape
+def correct(state_in, coarse_in, old_in, ends, result, S, N, O, E, Q, WP, in_sem, out_sem):
+    R, _, L, W = S.shape
     C, WCO = R // 2, W // 2
-
-    @pl.when(pl.program_id(0) == 0)
-    def _():
-        WP[...] = jnp.where((iota((WCO, W), 1) >> 1) == iota((WCO, W), 0), 1.0, 0.0).astype(jnp.bfloat16)
-
-    new = coarse_new[:, 0]
-    result[0] = jnp.swapaxes(new, 0, 1)
-    change = new - jnp.swapaxes(coarse_old[0], 0, 1)
-    change = picked(change.reshape(C * L, WCO), WP[...]).reshape(C, L, W)
-    for b in range(R // 8):
-        rows = jnp.stack([state[8 * b + i, 0] + change[4 * b + i // 2] for i in range(8)])
-        ends[0, :, pl.ds(8 * b, 8), :] = jnp.swapaxes(rows, 0, 1)
+    fetches = []
+    for f in range(3):
+        for i, (source, target) in enumerate(((coarse_in.at[:, f], N.at[:, f]), (old_in.at[f], O.at[f]),
+                                              (state_in.at[:, f], S.at[:, f]))):
+            fetches.append(pltpu.make_async_copy(source, target, in_sem.at[f, i]))
+            fetches[-1].start()
+    WP[...] = jnp.where((iota((WCO, W), 1) >> 1) == iota((WCO, W), 0), 1.0, 0.0).astype(jnp.bfloat16)
+    stores = []
+    for f in range(3):
+        fetches[3 * f].wait()
+        fetches[3 * f + 1].wait()
+        new = N[:, f]
+        Q[f] = jnp.swapaxes(new, 0, 1)
+        change = new - jnp.swapaxes(O[f], 0, 1)
+        change = picked(change.reshape(C * L, WCO), WP[...]).reshape(C, L, W)
+        fetches[3 * f + 2].wait()
+        for b in range(R // 8):
+            rows = jnp.stack([S[8 * b + i, f] + change[4 * b + i // 2] for i in range(8)])
+            E[f, :, pl.ds(8 * b, 8), :] = jnp.swapaxes(rows, 0, 1)
+        for i, (source, target) in enumerate(((E.at[f], ends.at[f]), (Q.at[f], result.at[f]))):
+            stores.append(pltpu.make_async_copy(source, target, out_sem.at[f, i]))
+            stores[-1].start()
+    for store in stores:
+        store.wait()
 
 
 def local(NT, NL, starts, coarse_old, mean_depth, coupling, wet_cells):
@@ -562,15 +580,12 @@
     )(starts[0], coarse_old[0], mean_depth, coupling, wet_cells)
     ends, result = pl.pallas_call(
         correct,
-        grid=(3,),
         out_shape=(jax.ShapeDtypeStruct((3, L, R, W), F32), jax.ShapeDtypeStruct((3, L, C, WCO), F32)),
-        in_specs=[
-            pl.BlockSpec((R, 1, L, W), lambda f: (0, f, 0, 0)),
-            pl.BlockSpec((C, 1, L, WCO), lambda f: (0, f, 0, 0)),
-            pl.BlockSpec((1, L, C, WCO), lambda f: (f, 0, 0, 0)),
-        ],
-        out_specs=(pl.BlockSpec((1, L, R, W), lambda f: (f, 0, 0, 0)), pl.BlockSpec((1, L, C, WCO), lambda f: (f, 0, 0, 0))),
-        scratch_shapes=[pltpu.VMEM((WCO, W), jnp.bfloat16)],
+        in_specs=[far] * 3,
+        out_specs=(far, far),
+        scratch_shapes=[
+            vmem(R, 3, L, W), vmem(C, 3, L, WCO), vmem(3, L, C, WCO), vmem(3, L, R, W), vmem(3, L, C, WCO),
+            half(WCO, W), sems(3, 3), sems(3, 2)],
         compiler_params=pltpu.CompilerParams(vmem_limit_bytes=63 * 1024 * 1024),
     )(state, coarse_new, coarse_old[0])
     return ends[None], result[None]

time: 56.1 us -> 54.6 us (0.973)
  Pallas kernels: 55.3 us -> 53.8 us
    pallas_call x1, Pallas kernels: 3.4 us -> 2.53 us  [local(): pl.pallas_call(correct, out_shape=(jax.ShapeDtypeStruct((3, L, R, W), F32...]
    pallas_call x1, Pallas kernels: 51.9 us -> 51.3 us  [local(): pl.pallas_call(functools.partial(kernel, NT, NL), out_shape=(jax.ShapeDty...]
where the time goes in v3:
time: 54.6 us; the launch traced here: 54.5 us
  Pallas kernels  53.8 us (99%)
  between operations  0.64 us (1%)
    pallas_call x1, Pallas kernels, local(): pl.pallas_call(functools.partial(kernel, NT, NL), out_shape=(jax.ShapeDty...  51.3 us
    pallas_call x1, Pallas kernels, local(): pl.pallas_call(correct, out_shape=(jax.ShapeDtypeStruct((3, L, R, W), F32...  2.53 us

profile of v3, /device:TPU:30, one launch (start us, length us, event | category | flops | bytes accessed | tf_op | source)
XLA Modules:
  0.0 54.5 jit_solution(16392082424790544674)
XLA Ops:
  0.6 51.3 %shard_map.68 = (f32[16,3,8,512]{3,2,1,0:T(8,128)}, f32[8,3,8,256]{3,2,1,0:T(8,128)}) custom-call(f32[3,8,16,512]{3,2,1,0:T(8,128)} %bitcast.6, f32[3,8,8,256]{3,2,1,0:T(8,128)} %bitcast.4, f32[8]{0:T(128)} %depth_in.1, f32[8,8]{1,0:T(8,128)} %coupling_in.1, s32[16,512]{1,0:T(8,128)} %wet_in.1), custom_call_target="tpu_custom_call" | custom-call | tf_op jit(solution)/shard_map/pallas_call | solution.py:559
  51.9 2.5 %shard_map.69 = (f32[3,8,16,512]{3,2,1,0:T(8,128)}, f32[3,8,8,256]{3,2,1,0:T(8,128)}) custom-call(f32[16,3,8,512]{3,2,1,0:T(8,128)} %get-tuple-element.6.state_in, f32[8,3,8,256]{3,2,1,0:T(8,128)} %get-tuple-element.7.coarse_in, f32[3,8,8,256]{3,2,1,0:T(8,128)} %bitcast.5), custom_call_target="tpu_custom_call" | custom-call | tf_op jit(solution)/shard_map/pallas_call | solution.py:581

commit v4 on v3

--- a/solution.py
+++ b/solution.py
@@ -87,8 +87,8 @@
     return out
 
 
-def kernel(NT, NL, starts_in, old_in, depth_in, coupling_in, wet_in, ends, coarse_new,
-           SV, OV, CV, WV, DS, DP, CF, in_sem, YA, Y1, Y2, PB, WET, WX, HB, KF, KC, WW, W2, WR, DL, TX, RX, TC, RC, CT, PC, WC, RES,
+def kernel(NT, NL, starts_in, old_in, depth_in, coupling_in, wet_in, ends, RC,
+           SV, OV, CV, WV, DS, DP, CF, in_sem, YA, Y1, Y2, PB, WET, WX, HB, KF, KC, WW, W2, WR, DL, TX, RX, TC, PK, CT, PC, WC, RES,
            CO, BW, CN, C0, P0, W0,
            hs_send, hs_recv, wx_send, wx_recv, tx_send, rx_recv, fw_send, fw_recv, tc_send, rc_recv):
     starts, coarse_old, mean_depth, coupling, wet_cells = SV, OV, DS, CV, WV
@@ -272,6 +272,19 @@
 
     HU = RC_ROWS // 2
     lanes = iota((L, 128), 1)
+    group = lanes // SLAB
+
+    def side_by_side(parts):
+        packed = parts[0]
+        for g in range(1, 4):
+            packed = jnp.where(group == g, parts[g], packed)
+        return packed
+
+    def own_result(source):
+        return pltpu.make_async_copy(source, RC.at[n], in_sem.at[8])
+
+    def first_result():
+        return pltpu.make_async_copy(PK, RC, in_sem.at[8])
 
     def slot_of(unit):
         return {1: 0, 2: 1, 0: 2, 3: 3}[unit]
@@ -398,6 +411,13 @@
             @pl.when(n == 0)
             def _():
                 coarse_first()
+                for m in range(NT):
+                    at = SLAB * m // 128 * 128
+                    for b in range(2):
+                        for i in range(3):
+                            PK[m, b, i] = side_by_side([
+                                rolled(CN[4 * b + g, i, :, pl.ds(at, 128)], SLAB * g - (SLAB * m - at)) for g in range(4)])
+                first_result().start()
                 BW[...] = picked((CN[...] - CO[...]).reshape(-1, WCO), W2[...])
 
             @pl.when(n > 0)
@@ -450,7 +470,6 @@
             device_id=(m, q), device_id_type=MESH)
 
     depth = depth_of(128)
-    group = lanes // SLAB
     for s in range(1, NT):
         now, later = CT.at[(s - 1) % 2], CT.at[s % 2]
         h = NT - 1 - s
@@ -475,10 +494,7 @@
                     later[r, i] = new[i] + row_of(s, r, i)
         for b in range(2):
             for i in range(3):
-                packed = rolled(RES[4 * b, i], -16)
-                for g in range(1, 4):
-                    packed = jnp.where(group == g, rolled(RES[4 * b + g, i], SLAB * g - 16), packed)
-                TC[s, b, i] = packed
+                TC[s, b, i] = side_by_side([rolled(RES[4 * b + g, i], SLAB * g - 16) for g in range(4)])
 
         @pl.when(n != s)
         def _(s=s):
@@ -486,7 +502,7 @@
 
         @pl.when(n == s)
         def _(s=s):
-            RC[s] = TC[s]
+            own_result(TC.at[s]).start()
 
     @pl.when(n > 0)
     def _():
@@ -494,16 +510,12 @@
         def _(j):
             result_arrival(lax.rem(n + j, NT)).wait_recv()
 
-        for r in range(RC_ROWS):
-            b, g = r // 4, r % 4
-            for i in range(3):
-                for j in range(WCO // 128):
-                    value = rolled(RC[4 * j, b, i], -SLAB * g)
-                    for m in range(1, 4):
-                        value = jnp.where(group == m, rolled(RC[4 * j + m, b, i], SLAB * (m - g)), value)
-                    CN[r, i, :, pl.ds(128 * j, 128)] = value
-
-    coarse_new[...] = CN[...]
+        own_result(TC.at[n]).wait()
+
+    @pl.when(n == 0)
+    def _():
+        first_result().wait()
+
     keep.wait()
     for phase in range(2):
         for_deltas(phase, lambda copy: copy.wait_send())
@@ -520,9 +532,11 @@
 def correct(state_in, coarse_in, old_in, ends, result, S, N, O, E, Q, WP, in_sem, out_sem):
     R, _, L, W = S.shape
     C, WCO = R // 2, W // 2
+    SLAB = WCO // N.shape[0]
+    group = iota((L, 128), 1) // SLAB
     fetches = []
     for f in range(3):
-        for i, (source, target) in enumerate(((coarse_in.at[:, f], N.at[:, f]), (old_in.at[f], O.at[f]),
+        for i, (source, target) in enumerate(((coarse_in.at[:, :, f], N.at[:, :, f]), (old_in.at[f], O.at[f]),
                                               (state_in.at[:, f], S.at[:, f]))):
             fetches.append(pltpu.make_async_copy(source, target, in_sem.at[f, i]))
             fetches[-1].start()
@@ -531,7 +545,16 @@
     for f in range(3):
         fetches[3 * f].wait()
         fetches[3 * f + 1].wait()
-        new = N[:, f]
+        rows = []
+        for r in range(C):
+            parts = []
+            for j in range(WCO // 128):
+                value = rolled(N[4 * j, r // 4, f], -SLAB * (r % 4))
+                for m in range(1, 4):
+                    value = jnp.where(group == m, rolled(N[4 * j + m, r // 4, f], SLAB * (m - r % 4)), value)
+                parts.append(value)
+            rows.append(jnp.concatenate(parts, axis=1))
+        new = jnp.stack(rows)
         Q[f] = jnp.swapaxes(new, 0, 1)
         change = new - jnp.swapaxes(O[f], 0, 1)
         change = picked(change.reshape(C * L, WCO), WP[...]).reshape(C, L, W)
@@ -554,16 +577,15 @@
     vmem = lambda *shape: pltpu.VMEM(shape, F32)
     half = lambda *shape: pltpu.VMEM(shape, jnp.bfloat16)
     sems = lambda *shape: pltpu.SemaphoreType.DMA(shape)
-    space = pl.BlockSpec(memory_space=pltpu.VMEM)
     far = pl.BlockSpec(memory_space=pltpu.HBM)
     state, coarse_new = pl.pallas_call(
         functools.partial(kernel, NT, NL),
-        out_shape=(jax.ShapeDtypeStruct((R, 3, L, W), F32), jax.ShapeDtypeStruct((C, 3, L, WCO), F32)),
+        out_shape=(jax.ShapeDtypeStruct((R, 3, L, W), F32), jax.ShapeDtypeStruct((NT, 2, 3, L, 128), F32)),
         in_specs=[far] * 5,
-        out_specs=(far, space),
+        out_specs=(far, far),
         scratch_shapes=[
             vmem(3, L, R, W), vmem(3, L, C, WCO), vmem(L, L), pltpu.VMEM((R, W), jnp.int32), pltpu.SMEM((L,), F32),
-            vmem(L, 128), vmem(L, L, 128), sems(8),
+            vmem(L, 128), vmem(L, L, 128), sems(9),
             vmem(E, 3, L, W), vmem(E, 3, L, W), vmem(E, 3, L, W), vmem(3, E, L, W), vmem(E, L, W),
             pltpu.VMEM((2, R, W), jnp.int32), vmem(STEPS, 2, HALO, 3, L, W),
             vmem(3 * C * L, 3 * C * L), vmem(3 * C * L, 3 * C * L),
@@ -584,7 +606,7 @@
         in_specs=[far] * 3,
         out_specs=(far, far),
         scratch_shapes=[
-            vmem(R, 3, L, W), vmem(C, 3, L, WCO), vmem(3, L, C, WCO), vmem(3, L, R, W), vmem(3, L, C, WCO),
+            vmem(R, 3, L, W), vmem(NT, 2, 3, L, 128), vmem(3, L, C, WCO), vmem(3, L, R, W), vmem(3, L, C, WCO),
             half(WCO, W), sems(3, 3), sems(3, 2)],
         compiler_params=pltpu.CompilerParams(vmem_limit_bytes=63 * 1024 * 1024),
     )(state, coarse_new, coarse_old[0])

time: 54.6 us -> 53.9 us (0.987)
  Pallas kernels: 53.8 us -> 53.2 us
    pallas_call x1, Pallas kernels: 51.3 us -> 50.5 us  [local(): pl.pallas_call(functools.partial(kernel, NT, NL), out_shape=(jax.ShapeDty...]
where the time goes in v4:
time: 53.9 us; the launch traced here: 53.8 us
  Pallas kernels  53.2 us (99%)
  between operations  0.64 us (1%)
    pallas_call x1, Pallas kernels, local(): pl.pallas_call(functools.partial(kernel, NT, NL), out_shape=(jax.ShapeDty...  50.5 us
    pallas_call x1, Pallas kernels, local(): pl.pallas_call(correct, out_shape=(jax.ShapeDtypeStruct((3, L, R, W), F32...  2.75 us

profile of v4, /device:TPU:30, one launch (start us, length us, event | category | flops | bytes accessed | tf_op | source)
XLA Modules:
  0.0 53.8 jit_solution(13626173491091546030)
XLA Ops:
  0.6 50.5 %shard_map.68 = (f32[16,3,8,512]{3,2,1,0:T(8,128)}, f32[8,2,3,8,128]{4,3,2,1,0:T(8,128)}) custom-call(f32[3,8,16,512]{3,2,1,0:T(8,128)} %bitcast.6, f32[3,8,8,256]{3,2,1,0:T(8,128)} %bitcast.4, f32[8]{0:T(128)} %depth_in.1, f32[8,8]{1,0:T(8,128)} %coupling_in.1, s32[16,512]{1,0:T(8,128)} %wet_in.1), custom_call_target="tpu_custom_call" | custom-call | tf_op jit(solution)/shard_map/pallas_call | solution.py:581
  51.1 2.7 %shard_map.69 = (f32[3,8,16,512]{3,2,1,0:T(8,128)}, f32[3,8,8,256]{3,2,1,0:T(8,128)}) custom-call(f32[16,3,8,512]{3,2,1,0:T(8,128)} %get-tuple-element.6.state_in, f32[8,2,3,8,128]{4,3,2,1,0:T(8,128)} %get-tuple-element.7.coarse_in, f32[3,8,8,256]{3,2,1,0:T(8,128)} %bitcast.5), custom_call_target="tpu_custom_call" | custom-call | tf_op jit(solution)/shard_map/pallas_call | solution.py:603

commit v5 on v4

--- a/solution.py
+++ b/solution.py
@@ -427,8 +427,16 @@
     keep = pltpu.make_async_copy(YA.at[pl.ds(HALO, R)], ends, in_sem.at[5 + 2])
     keep.start()
     deltas((0, 3))
-    send_deltas(1)
+    @pl.when(n <= 2)
+    def _():
+        send_deltas(1)
+
     pass_deltas(0)
+
+    @pl.when(n > 2)
+    def _():
+        send_deltas(1)
+
 
     E = 3 * RC_ROWS
     col = iota((W, 128), 1)
@@ -480,8 +488,6 @@
             for shift in range(1, L):
                 total = total + (0.5 * CF[shift]) * pltpu.roll(e, shift, axis=0)
             PC[r] = total
-        if s < NT - 1:
-            arrived(s)
         for r in range(lo, hi):
             row = q * RC_ROWS + (r - RC_ROWS)
             f = rotation * (2.0 * (row.astype(F32) + 0.5) / (RC_ROWS * NL) - 1.0)
@@ -491,7 +497,7 @@
                 if RC_ROWS <= r < 2 * RC_ROWS:
                     RES[r - RC_ROWS, i] = new[i]
                 if s < NT - 1:
-                    later[r, i] = new[i] + row_of(s, r, i)
+                    later[r, i] = new[i]
         for b in range(2):
             for i in range(3):
                 TC[s, b, i] = side_by_side([rolled(RES[4 * b + g, i], SLAB * g - 16) for g in range(4)])
@@ -503,6 +509,12 @@
         @pl.when(n == s)
         def _(s=s):
             own_result(TC.at[s]).start()
+
+        if s < NT - 1:
+            arrived(s)
+            for r in range(lo, hi):
+                for i in range(3):
+                    later[r, i] = later[r, i] + row_of(s, r, i)
 
     @pl.when(n > 0)
     def _():

time: 53.9 us -> 53.2 us (0.987)
  Pallas kernels: 53.2 us -> 52.5 us
    pallas_call x1, Pallas kernels: 50.5 us -> 49.7 us  [local(): pl.pallas_call(functools.partial(kernel, NT, NL), out_shape=(jax.ShapeDty...]
where the time goes in v5:
time: 53.2 us; the launch traced here: 53.1 us
  Pallas kernels  52.5 us (99%)
  between operations  0.64 us (1%)
    pallas_call x1, Pallas kernels, local(): pl.pallas_call(functools.partial(kernel, NT, NL), out_shape=(jax.ShapeDty...  49.7 us
    pallas_call x1, Pallas kernels, local(): pl.pallas_call(correct, out_shape=(jax.ShapeDtypeStruct((3, L, R, W), F32...  2.75 us

profile of v5, /device:TPU:30, one launch (start us, length us, event | category | flops | bytes accessed | tf_op | source)
XLA Modules:
  0.0 53.1 jit_solution(9597145091223701584)
XLA Ops:
  0.6 49.7 %shard_map.68 = (f32[16,3,8,512]{3,2,1,0:T(8,128)}, f32[8,2,3,8,128]{4,3,2,1,0:T(8,128)}) custom-call(f32[3,8,16,512]{3,2,1,0:T(8,128)} %bitcast.6, f32[3,8,8,256]{3,2,1,0:T(8,128)} %bitcast.4, f32[8]{0:T(128)} %depth_in.1, f32[8,8]{1,0:T(8,128)} %coupling_in.1, s32[16,512]{1,0:T(8,128)} %wet_in.1), custom_call_target="tpu_custom_call" | custom-call | tf_op jit(solution)/shard_map/pallas_call | solution.py:593
  50.4 2.7 %shard_map.69 = (f32[3,8,16,512]{3,2,1,0:T(8,128)}, f32[3,8,8,256]{3,2,1,0:T(8,128)}) custom-call(f32[16,3,8,512]{3,2,1,0:T(8,128)} %get-tuple-element.6.state_in, f32[8,2,3,8,128]{4,3,2,1,0:T(8,128)} %get-tuple-element.7.coarse_in, f32[3,8,8,256]{3,2,1,0:T(8,128)} %bitcast.5), custom_call_target="tpu_custom_call" | custom-call | tf_op jit(solution)/shard_map/pallas_call | solution.py:615

commit v6 on v5

--- a/solution.py
+++ b/solution.py
@@ -425,7 +425,6 @@
                 BW[...] = picked((-CO[...]).reshape(-1, WCO), W2[...])
 
     keep = pltpu.make_async_copy(YA.at[pl.ds(HALO, R)], ends, in_sem.at[5 + 2])
-    keep.start()
     deltas((0, 3))
     @pl.when(n <= 2)
     def _():
@@ -449,6 +448,7 @@
             WC[part * RC_ROWS + i] = jnp.broadcast_to(window[i:i + 1, :], (L, 128))
 
     pass_deltas(1)
+    keep.start()
 
     def arrived(s):
         for phase in range(2):

time: 53.2 us -> 53.2 us (level)
  no operation moved by 1% of the time
where the time goes in v6:
time: 53.2 us; the launch traced here: 53.1 us
  Pallas kernels  52.5 us (99%)
  between operations  0.64 us (1%)
    pallas_call x1, Pallas kernels, local(): pl.pallas_call(functools.partial(kernel, NT, NL), out_shape=(jax.ShapeDty...  49.7 us
    pallas_call x1, Pallas kernels, local(): pl.pallas_call(correct, out_shape=(jax.ShapeDtypeStruct((3, L, R, W), F32...  2.75 us

profile of v6, /device:TPU:30, one launch (start us, length us, event | category | flops | bytes accessed | tf_op | source)
XLA Modules:
  0.0 53.1 jit_solution(17143755386723136665)
XLA Ops:
  0.6 49.7 %shard_map.68 = (f32[16,3,8,512]{3,2,1,0:T(8,128)}, f32[8,2,3,8,128]{4,3,2,1,0:T(8,128)}) custom-call(f32[3,8,16,512]{3,2,1,0:T(8,128)} %bitcast.6, f32[3,8,8,256]{3,2,1,0:T(8,128)} %bitcast.4, f32[8]{0:T(128)} %depth_in.1, f32[8,8]{1,0:T(8,128)} %coupling_in.1, s32[16,512]{1,0:T(8,128)} %wet_in.1), custom_call_target="tpu_custom_call" | custom-call | tf_op jit(solution)/shard_map/pallas_call | solution.py:593
  50.4 2.7 %shard_map.69 = (f32[3,8,16,512]{3,2,1,0:T(8,128)}, f32[3,8,8,256]{3,2,1,0:T(8,128)}) custom-call(f32[16,3,8,512]{3,2,1,0:T(8,128)} %get-tuple-element.6.state_in, f32[8,2,3,8,128]{4,3,2,1,0:T(8,128)} %get-tuple-element.7.coarse_in, f32[3,8,8,256]{3,2,1,0:T(8,128)} %bitcast.5), custom_call_target="tpu_custom_call" | custom-call | tf_op jit(solution)/shard_map/pallas_call | solution.py:615
